TPU v7x, 128 devices: a whole 4x4x4 slice. The times are simulated.
128 devices in a mesh: lon: 16 (over y_hi, z, core), lat: 8 (over y_lo, x).
Axes of the slice: x: 4, y: 4 (y_hi: 2, y_lo: 2; y = y_hi * 2 + y_lo), z: 4, core: 2. Of those that a mesh axis runs over, the one named last changes fastest.
Arguments:
- fields: bfloat16 [4, 48, 384, 192], P(None, 'lat', 'lon'), may hold values from -6 to 6
- cotangent: bfloat16 [4, 48, 384, 192], P(None, 'lat', 'lon'), may hold values from -6 to 6
- bias_table: float32 [8, 2, 6, 3312], P('lat'), may hold values from -4 to 310
- gain_one: float32 [192], replicated, may hold values from 0.5 to 1.5
- w_qkv: bfloat16 [192, 576], replicated, may hold values from -2 to 2
- w_proj: bfloat16 [192, 192], replicated, may hold values from -0.4375 to 0.4375
- gain_two: float32 [192], replicated, may hold values from 0.5 to 1.5
- w_in: bfloat16 [192, 768], replicated, may hold values from -0.4375 to 0.4375
- w_out: bfloat16 [768, 192], replicated, may hold values from -0.21875 to 0.21875
Outputs:
- block_out: bfloat16 [4, 48, 384, 192], P(None, 'lat', 'lon')
- grad_fields: bfloat16 [4, 48, 384, 192], P(None, 'lat', 'lon')
- grad_gain_one: float32 [192], replicated
- grad_w_qkv: float32 [192, 576], replicated
- grad_table: float32 [8, 2, 6, 3312], P('lat')
- grad_w_proj: float32 [192, 192], replicated
- grad_gain_two: float32 [192], replicated
- grad_w_in: float32 [192, 768], replicated
- grad_w_out: float32 [768, 192], replicated
All inputs are finite; a program needn't handle non-finite values.
Results may differ from a plain program's by a relative error of at most 0.012.
Values may be sent and summed in bfloat16 or wider, within the bound.
A program may use at most 128 MiB of HBM per device.

v0:
```python
import jax
import jax.numpy as jnp
from jax import lax
from jax.sharding import PartitionSpec as P

HEADS = 6


def shifted(value, axis, steps):
    count = lax.axis_size(axis)
    pairs = [(source, (source + steps) % count) for source in range(count)]
    return lax.ppermute(value, axis, pairs)


def contract(formula, left_op, right_op):
    return jnp.einsum(formula, left_op, right_op, preferred_element_type=jnp.float32)


def weight_grad(left_op, right_op):
    return lax.dot_general(
        left_op, right_op, (((0,), (0,)), ((), ())), preferred_element_type=jnp.float32
    )


def layer_norm(values, gain_vec):
    center = values - jnp.mean(values, axis=-1, keepdims=True)
    spread = jnp.mean(center * center, axis=-1, keepdims=True)
    return center * lax.rsqrt(spread + 1e-05) * gain_vec


def gelu_exact(values):
    return jax.nn.gelu(values, approximate=False)


def offset_table():
    offsets = lax.broadcasted_iota(jnp.int32, (23, 12, 12), 0)
    first_col = lax.broadcasted_iota(jnp.int32, (23, 12, 12), 1)
    second_col = lax.broadcasted_iota(jnp.int32, (23, 12, 12), 2)
    return (offsets == first_col - second_col + 11).astype(jnp.float32)


def to_windows(grid_cells):
    levels, lat_rows, lon_cols, feat_dim = grid_cells.shape
    blocks = grid_cells.reshape(levels // 2, 2, lat_rows // 6, 6, lon_cols // 12, 12, feat_dim)
    blocks = blocks.transpose(2, 0, 4, 1, 3, 5, 6)
    return blocks.reshape(lat_rows // 6, levels // 2, lon_cols // 12, 144, feat_dim)


def from_windows(blocks, levels, lat_rows, lon_cols):
    feat_dim = blocks.shape[-1]
    grid_cells = blocks.reshape(lat_rows // 6, levels // 2, lon_cols // 12, 2, 6, 12, feat_dim)
    return grid_cells.transpose(1, 3, 0, 4, 2, 5, 6).reshape(levels, lat_rows, lon_cols, feat_dim)


def block_pass(
    fields, cotangent, lat_wrap, bias_table, gain_one, w_qkv, w_proj, gain_two, w_in, w_out
):
    levels, lat_rows, lon_cols, width = fields.shape
    depth_dim = width // HEADS
    flat_in = fields.reshape(-1, width).astype(jnp.float32)
    normed_one = layer_norm(flat_in, gain_one).astype(jnp.bfloat16)
    qkv_flat = jnp.dot(normed_one, w_qkv, preferred_element_type=jnp.float32).astype(jnp.bfloat16)
    level_ids = lax.broadcasted_iota(jnp.int32, (levels, lat_rows, lon_cols, 1), 0)
    wrap_ids = jnp.broadcast_to(
        lat_wrap.reshape(1, lat_rows, 1, 1), (levels, lat_rows, lon_cols, 1)
    )
    region = to_windows((level_ids == levels - 1).astype(jnp.int32) * 2 + wrap_ids)[..., 0]
    windows = to_windows(qkv_flat.reshape(levels, lat_rows, lon_cols, 3 * width))
    win_rows, win_levels, win_cols = (windows.shape[0], windows.shape[1], windows.shape[2])
    qkv_parts = windows.reshape(win_rows, win_levels, win_cols, 144, 3, HEADS, depth_dim)
    queries = qkv_parts[:, :, :, :, 0]
    key_vecs = qkv_parts[:, :, :, :, 1]
    values = qkv_parts[:, :, :, :, 2]
    score_scale = depth_dim ** (-0.5)
    spread_table = offset_table()
    scores = contract("abcihd,abcjhd->abchij", queries, key_vecs) * score_scale
    table_parts = bias_table.reshape(win_rows, win_levels, HEADS, 2, 2, 6, 6, 23)
    pos_bias = jnp.einsum(
        "rlhabcdo,oxy->rlhacxbdy", table_parts, spread_table, precision=lax.Precision.HIGHEST
    )
    pos_bias = pos_bias.reshape(win_rows, win_levels, 1, HEADS, 144, 144)
    same_region = (region[:, :, :, :, None] == region[:, :, :, None, :])[:, :, :, None]
    scores = jnp.where(same_region, scores + pos_bias, -1000000000.0)
    row_max = jnp.max(scores, axis=-1, keepdims=True)
    exp_scores = jnp.exp(scores - row_max)
    attn_probs = exp_scores / jnp.sum(exp_scores, axis=-1, keepdims=True)
    probs_b = attn_probs.astype(jnp.bfloat16)
    mixed_heads = contract("abchij,abcjhd->abcihd", probs_b, values).astype(jnp.bfloat16)
    attended = from_windows(
        mixed_heads.reshape(win_rows, win_levels, win_cols, 144, width), levels, lat_rows, lon_cols
    ).reshape(-1, width)
    branch = flat_in + jnp.dot(attended, w_proj, preferred_element_type=jnp.float32)
    normed_two = layer_norm(branch, gain_two).astype(jnp.bfloat16)
    pre_act = jnp.dot(normed_two, w_in, preferred_element_type=jnp.float32)
    act_full, gelu_back = jax.vjp(gelu_exact, pre_act)
    act_b = act_full.astype(jnp.bfloat16)
    block_out = (
        (branch + jnp.dot(act_b, w_out, preferred_element_type=jnp.float32))
        .astype(jnp.bfloat16)
        .reshape(fields.shape)
    )
    grad_out = cotangent.reshape(-1, width)
    g_w_out = weight_grad(act_b, grad_out)
    d_act = jnp.dot(grad_out, w_out.T, preferred_element_type=jnp.float32)
    d_pre = gelu_back(d_act)[0].astype(jnp.bfloat16)
    g_w_in = weight_grad(normed_two, d_pre)
    d_normed_two = jnp.dot(d_pre, w_in.T, preferred_element_type=jnp.float32)
    unused_two, second_back = jax.vjp(layer_norm, branch, gain_two)
    d_branch_norm, g_gain_two = second_back(d_normed_two)
    d_branch = grad_out.astype(jnp.float32) + d_branch_norm
    d_branch_b = d_branch.astype(jnp.bfloat16)
    g_w_proj = weight_grad(attended, d_branch_b)
    d_attended = jnp.dot(d_branch_b, w_proj.T, preferred_element_type=jnp.float32).astype(
        jnp.bfloat16
    )
    d_mixed = to_windows(d_attended.reshape(levels, lat_rows, lon_cols, width)).reshape(
        win_rows, win_levels, win_cols, 144, HEADS, depth_dim
    )
    d_probs = contract("abcihd,abcjhd->abchij", d_mixed, values)
    d_values = contract("abchij,abcihd->abcjhd", probs_b, d_mixed).astype(jnp.bfloat16)
    d_scores = attn_probs * (d_probs - jnp.sum(d_probs * attn_probs, axis=-1, keepdims=True))
    d_bias = jnp.sum(d_scores, axis=2).reshape(win_rows, win_levels, HEADS, 2, 6, 12, 2, 6, 12)
    g_table = jnp.einsum(
        "rlhacxbdy,oxy->rlhabcdo", d_bias, spread_table, precision=lax.Precision.HIGHEST
    )
    g_table = g_table.reshape(win_rows, win_levels, HEADS, bias_table.shape[3])
    d_scores_b = d_scores.astype(jnp.bfloat16)
    d_queries = (contract("abchij,abcjhd->abcihd", d_scores_b, key_vecs) * score_scale).astype(
        jnp.bfloat16
    )
    d_keys = (contract("abchij,abcihd->abcjhd", d_scores_b, queries) * score_scale).astype(
        jnp.bfloat16
    )
    d_windows = jnp.stack([d_queries, d_keys, d_values], axis=4).reshape(
        win_rows, win_levels, win_cols, 144, 3 * width
    )
    d_qkv = from_windows(d_windows, levels, lat_rows, lon_cols).reshape(-1, 3 * width)
    g_w_qkv = weight_grad(normed_one, d_qkv)
    d_normed_one = jnp.dot(d_qkv, w_qkv.T, preferred_element_type=jnp.float32)
    unused_one, first_back = jax.vjp(layer_norm, flat_in, gain_one)
    d_input, g_gain_one = first_back(d_normed_one)
    grad_fields = (d_branch + d_input).astype(jnp.bfloat16).reshape(fields.shape)
    return (
        block_out,
        grad_fields,
        (g_gain_one, g_w_qkv, g_table, g_w_proj, g_gain_two, g_w_in, g_w_out),
    )


def local(fields, cotangent, bias_table, gain_one, w_qkv, w_proj, gain_two, w_in, w_out):
    lat_rows = fields.shape[1]
    top_field, top_cot = shifted((fields[:, :3], cotangent[:, :3]), "lat", -1)
    lat_field = jnp.concatenate([fields[:, 3:], top_field], axis=1)
    lat_cot = jnp.concatenate([cotangent[:, 3:], top_cot], axis=1)
    side_field, side_cot = shifted((lat_field[:, :, :6], lat_cot[:, :, :6]), "lon", -1)
    shifted_in = jnp.roll(jnp.concatenate([lat_field[:, :, 6:], side_field], axis=2), -1, axis=0)
    shifted_cot = jnp.roll(jnp.concatenate([lat_cot[:, :, 6:], side_cot], axis=2), -1, axis=0)
    last_band = lax.axis_index("lat") == lax.axis_size("lat") - 1
    lat_wrap = jnp.logical_and(lax.iota(jnp.int32, lat_rows) >= lat_rows - 3, last_band).astype(
        jnp.int32
    )
    block_out, grad_fields, grads = block_pass(
        shifted_in,
        shifted_cot,
        lat_wrap,
        bias_table,
        gain_one,
        w_qkv,
        w_proj,
        gain_two,
        w_in,
        w_out,
    )
    out_back = jnp.roll(block_out, 1, axis=0)
    grad_back = jnp.roll(grad_fields, 1, axis=0)
    left_out, left_grad = shifted((out_back[:, :, -6:], grad_back[:, :, -6:]), "lon", 1)
    out_back = jnp.concatenate([left_out, out_back[:, :, :-6]], axis=2)
    grad_back = jnp.concatenate([left_grad, grad_back[:, :, :-6]], axis=2)
    upper_out, upper_grad = shifted((out_back[:, -3:], grad_back[:, -3:]), "lat", 1)
    out_back = jnp.concatenate([upper_out, out_back[:, :-3]], axis=1)
    grad_back = jnp.concatenate([upper_grad, grad_back[:, :-3]], axis=1)
    g_gain_one, g_w_qkv, g_table, g_w_proj, g_gain_two, g_w_in, g_w_out = grads
    summed = lax.psum((g_gain_one, g_w_qkv, g_w_proj, g_gain_two, g_w_in, g_w_out), ("lon", "lat"))
    table_total = lax.psum(g_table, "lon")
    return (
        out_back,
        grad_back,
        summed[0],
        summed[1],
        table_total,
        summed[2],
        summed[3],
        summed[4],
        summed[5],
    )


def solution(mesh):
    placed = (
        P(None, "lat", "lon", None),
        P(None, "lat", "lon", None),
        P("lat", None, None, None),
        P(),
        P(),
        P(),
        P(),
        P(),
        P(),
    )
    return jax.shard_map(
        local,
        mesh=mesh,
        in_specs=placed,
        out_specs=(
            P(None, "lat", "lon", None),
            P(None, "lat", "lon", None),
            P(),
            P(),
            P("lat", None, None, None),
            P(),
            P(),
            P(),
            P(),
        ),
        check_vma=False,
    )
```

profile of v0, /device:TPU:1, one launch (start us, length us, event | category | flops | bytes accessed | tf_op | source)
XLA Modules:
  0.0 476.6 jit_solution(2004558671525242351)
XLA Ops:
  7.2 1.0 fusion.71
  8.3 4.4 collective-permute-start
  12.7 1.0 fusion.69
  13.7 0.6 collective-permute-start.4
  14.5 0.8 broadcast_compare_fusion
  15.3 1.8 reshape.297
  17.1 8.8 %convolution_bitcast_fusion = f32[1,2,6,2,6,12,2,6,12]{8,7,4,6,3,2,1,5,0:T(8,128)} fusion(f32[2,6,2,2,6,6,23]{6,5,4,3,2,0,1:T(8,128)S(1)} %reshape.297), kind=kOutput, calls=%fused_computation.1 | convolution fusion | flops 68687568 | bytes 1154304 | tf_op jit(solution)/shard_map/rlhabcdo,oxy->rlhacxbdy/dot_general | solution.py:78
  25.8 20.6 %copy.94 = f32[1,2,6,2,6,12,2,6,12]{5,4,3,8,7,6,2,1,0:T(8,128)} copy(f32[1,2,6,2,6,12,2,6,12]{8,7,4,6,3,2,1,5,0:T(8,128)} %convolution_bitcast_fusion) | data formatting | bytes 1990656 | tf_op jit(solution)/shard_map/add | solution.py:83
  46.4 10.2 %reshape.306 = f32[2,6,144,144]{2,3,1,0:T(8,128)} reshape(f32[1,2,6,2,6,12,2,6,12]{5,4,3,8,7,6,2,1,0:T(8,128)} %copy.94) | data formatting | bytes 1990656 | tf_op jit(solution)/shard_map/add | solution.py:83
  56.7 1.3 collective-permute-start.1
  58.0 5.3 %collective-permute-start.5 = (bf16[4,6,6,192]{3,2,1,0:T(8,128)(2,1)S(1)}, bf16[4,6,6,192]{3,2,1,0:T(8,128)(2,1)S(1)}, u32[]{:S(2)}, u32[]{:S(2)}) collective-permute-start(bf16[4,6,6,192]{3,2,1,0:T(8,128)(2,1)S(1)} %pad_maximum_fusion.8), channel_id=1, source_target_pairs={{0,120},{8,0},{16,8},{24,16},{32,24},{40,32},{48,40},{56,48},{64,5... | collective-permute-start | bytes 165896 | tf_op jit(solution)/shard_map/ppermute | solution.py:12
  64.1 0.6 fusion.60
  65.1 0.9 copy.72
  66.9 0.6 copy.59
  67.5 4.3 reshape_reshape.23
  71.7 3.6 fusion.67
  75.3 2.7 copy.99
  78.0 1.5 copy.98
  79.6 0.8 copy.100
  80.4 5.0 %fusion.72 = (f32[2,2,6,144]{3,2,1,0:T(8,128)S(1)}, f32[2,2,6,144,144]{3,4,2,1,0:T(8,128)}) fusion(f32[2,6,144,144]{2,3,1,0:T(8,128)} %reshape.306, pred[2,2,144,144]{2,3,1,0:T(8,128)(4,1)} %broadcast_compare_fusion, bf16[1,2,2,144,1,6,32]{3,6,5,2,1,4,0:T(8,128)(2,1)S(1)} %copy.100, bf16[1,2,2,144,1,6,32]{3,6,5,2,1,4,0:T(8,128)(2,1)} %copy.99), kind=kOutput, calls=%fused_computation.135 | convolution fusion | flops 34338960 | bytes 3525120 | tf_op jit(solution)/shard_map/sub | solution.py:85
  85.4 2.4 fusion.16
  87.8 0.9 copy.67
  88.7 0.7 reshape_reshape.24
  90.1 4.0 multiply_convert_fusion
  94.2 1.3 fusion.80
  96.1 1.3 add_convert_fusion
  97.3 1.2 multiply_reduce_fusion.2
  98.5 1.3 fusion.62
  100.0 1.0 fusion.79
  101.8 0.6 reshape.299
  102.3 0.8 copy.75
  103.1 3.6 fusion.17
  106.7 0.8 multiply_reduce_fusion
  107.5 1.1 fusion.12
  108.6 0.6 fusion.18
  109.6 1.1 fusion.19
  110.7 0.9 multiply_convert_fusion.1
  111.9 0.7 pad_maximum_fusion.9
  112.6 2.4 pad_maximum_fusion
  115.0 5.1 %copy.80 = bf16[1,2,2,144,3,6,32]{6,5,4,2,3,1,0:T(8,128)(2,1)} copy(bf16[1,2,2,144,3,6,32]{3,6,5,2,1,4,0:T(8,128)(2,1)} %pad_maximum_fusion) | data formatting | bytes 1327104 | tf_op jit(solution)/shard_map/stack | solution.py:134
  120.1 5.2 %reshape_reshape.27 = bf16[1,2,2,2,6,12,576]{6,2,5,4,3,1,0:T(2,128)(2,1)S(1)} reshape(bf16[1,2,2,144,3,6,32]{6,5,4,2,3,1,0:T(8,128)(2,1)} %copy.80) | data formatting | bytes 1327104 | tf_op jit(solution)/shard_map/reshape;reshape | solution.py:51
  125.3 1.1 copy.81
  126.4 1.5 reshape_reshape.28
  127.9 1.5 multiply_reduce_fusion.4
  129.7 0.9 add_convert_fusion.1
  130.6 8.6 %reshape.307 = f32[2,6,2,6,12,2,6,12]{4,3,2,7,6,5,1,0:T(8,128)} reshape(f32[2,6,144,144]{2,3,1,0:T(8,128)S(1)} %get-tuple-element.25) | data formatting | bytes 1990656 | tf_op jit(solution)/shard_map/reshape.64
  139.2 20.1 %copy.85 = f32[2,6,2,6,12,2,6,12]{7,6,4,5,3,2,1,0:T(8,128)} copy(f32[2,6,2,6,12,2,6,12]{4,3,2,7,6,5,1,0:T(8,128)} %reshape.307) | data formatting | bytes 1990656 | tf_op jit(solution)/shard_map/reshape.64
  159.3 12.6 %convolution_bitcast_fusion.1 = f32[1,2,6,2,2,6,6,23]{7,6,4,5,3,2,1,0:T(8,128)S(1)} fusion(f32[2,6,2,6,12,2,6,12]{7,6,4,5,3,2,1,0:T(8,128)} %copy.85), kind=kOutput, calls=%fused_computation.29 | convolution fusion | flops 68687568 | bytes 1154304 | tf_op jit(solution)/shard_map/rlhacxbdy,oxy->rlhabcdo/dot_general | solution.py:123
  172.0 1.3 reshape.301
  173.4 1.2 fusion.78
  175.4 67.9 %all-reduce = (f32[192]{0:T(256)}, f32[192]{0:T(256)}) all-reduce(f32[192]{0:T(256)S(1)} %get-tuple-element.9, f32[192]{0:T(256)S(1)} %copy-done.35), channel_id=1, replica_groups=mesh['lon'=16,'lat'=8] {'lon','lat'}, use_global_device_ids=true, to_apply=%region_12.13 | all-reduce | flops 384 | bytes 3072 | tf_op jit(solution)/shard_map/psum | solution.py:183
  243.3 1.0 fusion.44
  244.4 0.9 collective-permute-start.3
  245.5 5.8 %collective-permute-done.3 = bf16[4,3,24,192]{3,2,1,0:T(8,128)(2,1)S(1)} collective-permute-done((bf16[4,3,24,192]{3,2,1,0:T(8,128)(2,1)S(1)}, bf16[4,3,24,192]{3,2,1,0:T(8,128)(2,1)S(1)}, u32[]{:S(2)}, u32[]{:S(2)}) %collective-permute-start.3) | collective-permute-done | bytes 110624 | tf_op jit(solution)/shard_map/ppermute | solution.py:12
  251.3 0.8 pad_maximum_fusion.5
  252.1 2.4 collective-permute-done.7
  254.5 0.8 pad_maximum_fusion.6
  255.2 47.6 %all-reduce.5.cloned.1.call-done = f32[1,2,6,3312]{3,1,2,0:T(2,128)} async-done(((f32[1,2,6,3312]{3,1,2,0:T(2,128)}), f32[1,2,6,3312]{3,1,2,0:T(2,128)}) %all-reduce.5.cloned.1.call-update) | async-done | bytes 158992 | tf_op jit(solution)/shard_map/psum | solution.py:184
  302.9 159.9 %all-reduce.7.cloned.1.call-done = (f32[192,576]{1,0:T(8,128)}, f32[192,192]{1,0:T(8,128)}, f32[192,768]{1,0:T(8,128)}, f32[768,192]{0,1:T(8,128)}) async-done(((f32[192,576]{1,0:T(8,128)}, f32[192,192]{1,0:T(8,128)}, f32[192,768]{1,0:T(8,128)}, f32[768,192]{0,1:T(8,128)}), (f32[192,576]{1,0:T(8,128)}, f32[192,192]{1,0:T(8,128)}, f32[192,768]{1,0:T(8,128)}, ...) | async-done | bytes 1769488 | tf_op jit(solution)/shard_map/psum | solution.py:183
  462.8 2.0 copy.110
  464.7 1.6 copy.111
  466.3 1.6 copy.112
  467.9 0.8 copy.113
  468.8 0.8 copy.114
  (137 shorter events, 6.4 us)
Async XLA Ops:
  7.2 82.9 %copy-start = (bf16[192,768]{1,0:T(8,128)(2,1)S(1)}, bf16[192,768]{1,0:T(8,128)(2,1)}, u32[]{:S(2)}) copy-start(bf16[192,768]{1,0:T(8,128)(2,1)} %param.16) | copy-start | bytes 884740
  7.2 295.7 %all-reduce.5.cloned.1.call-start = ((), (), s32[]{:S(2)}) async-start(), calls=%async_computation | async-start | bytes 319488 | tf_op jit(solution)/shard_map/psum | solution.py:184
  8.3 48.4 %collective-permute-start = (bf16[4,3,24,192]{3,2,1,0:T(8,128)(2,1)S(1)}, bf16[4,3,24,192]{3,2,1,0:T(8,128)(2,1)S(1)}, u32[]{:S(2)}, u32[]{:S(2)}) collective-permute-start(bf16[4,3,24,192]{3,2,1,0:T(8,128)(2,1)S(1)} %get-tuple-element.37), channel_id=1, source_target_pairs={{0,7},{1,0},{2,1},{3,2},{4,3},{5,4},{6,5},{7,6},{8,15},{9,8},{10,9... | collective-permute-start | bytes 331784 | tf_op jit(solution)/shard_map/ppermute | solution.py:12
  13.7 44.3 %collective-permute-start.4 = (bf16[4,3,24,192]{3,2,1,0:T(8,128)(2,1)S(1)}, bf16[4,3,24,192]{3,2,1,0:T(8,128)(2,1)S(1)}, u32[]{:S(2)}, u32[]{:S(2)}) collective-permute-start(bf16[4,3,24,192]{3,2,1,0:T(8,128)(2,1)S(1)} %get-tuple-element.33), channel_id=1, source_target_pairs={{0,7},{1,0},{2,1},{3,2},{4,3},{5,4},{6,5},{7,6},{8,15},{9,8},{10,9... | collective-permute-start | bytes 331784 | tf_op jit(solution)/shard_map/ppermute | solution.py:12
  56.7 6.8 %collective-permute-start.1 = (bf16[4,6,6,192]{3,2,1,0:T(8,128)(2,1)S(1)}, bf16[4,6,6,192]{3,2,1,0:T(8,128)(2,1)S(1)}, u32[]{:S(2)}, u32[]{:S(2)}) collective-permute-start(bf16[4,6,6,192]{3,2,1,0:T(8,128)(2,1)S(1)} %pad_maximum_fusion.10), channel_id=1, source_target_pairs={{0,120},{8,0},{16,8},{24,16},{32,24},{40,32},{48,40},{56,48},{64,5... | collective-permute-start | bytes 165896 | tf_op jit(solution)/shard_map/ppermute | solution.py:12
  58.0 6.9 %collective-permute-start.5 = (bf16[4,6,6,192]{3,2,1,0:T(8,128)(2,1)S(1)}, bf16[4,6,6,192]{3,2,1,0:T(8,128)(2,1)S(1)}, u32[]{:S(2)}, u32[]{:S(2)}) collective-permute-start(bf16[4,6,6,192]{3,2,1,0:T(8,128)(2,1)S(1)} %pad_maximum_fusion.8), channel_id=1, source_target_pairs={{0,120},{8,0},{16,8},{24,16},{32,24},{40,32},{48,40},{56,48},{64,5... | collective-permute-start | bytes 165896 | tf_op jit(solution)/shard_map/ppermute | solution.py:12
  63.8 2.3 copy-start.14
  63.8 2.3 copy-start.32
  64.8 1.9 copy-start.23
  64.9 1.8 copy-start.30
  64.9 1.8 copy-start.25
  65.1 0.9 copy-start.5
  80.4 5.0 %copy-start.10 = (bf16[1,2,2,144,1,6,32]{3,6,5,2,1,4,0:T(8,128)(2,1)}, bf16[1,2,2,144,1,6,32]{3,6,5,2,1,4,0:T(8,128)(2,1)S(1)}, u32[]{:S(2)}) copy-start(bf16[1,2,2,144,1,6,32]{3,6,5,2,1,4,0:T(8,128)(2,1)S(1)} %copy.100) | copy-start | bytes 663556
  80.4 5.0 %copy-start.19 = (bf16[1,2,2,144,1,6,32]{3,6,5,2,1,4,0:T(8,128)(2,1)S(1)}, bf16[1,2,2,144,1,6,32]{3,6,5,2,1,4,0:T(8,128)(2,1)}, u32[]{:S(2)}) copy-start(bf16[1,2,2,144,1,6,32]{3,6,5,2,1,4,0:T(8,128)(2,1)} %copy.98) | copy-start | bytes 663556
  88.7 1.0 copy-start.21
  89.4 0.7 copy-start.34
  90.1 4.1 copy-start.6
  94.2 1.3 copy-start.22
  98.5 1.5 copy-start.7
  99.9 1.6 copy-start.2
  100.0 1.1 copy-start.28
  103.1 3.6 copy-start.4
  103.1 3.6 copy-start.20
  107.5 1.1 copy-start.9
  108.6 1.0 copy-start.11
  109.6 1.1 copy-start.27
  109.6 1.1 copy-start.33
  111.8 3.2 copy-start.15
  112.6 130.7 %collective-permute-start.2 = (bf16[4,6,6,192]{3,2,1,0:T(8,128)(2,1)}, bf16[4,6,6,192]{3,2,1,0:T(8,128)(2,1)}, u32[]{:S(2)}, u32[]{:S(2)}) collective-permute-start(bf16[4,6,6,192]{3,2,1,0:T(8,128)(2,1)} %pad_maximum_fusion.9), channel_id=1, source_target_pairs={{0,8},{8,16},{16,24},{24,32},{32,40},{40,48},{48,56},{56,64},{64,7... | collective-permute-start | bytes 165896 | tf_op jit(solution)/shard_map/ppermute | solution.py:12
  125.3 2.6 copy-start.24
  126.4 3.0 copy-start.31
  126.4 3.1 copy-start.26
  127.9 1.8 copy-start.3
  127.9 1.8 copy-start.8
  127.9 1.8 copy-start.29
  171.9 1.5 copy-start.13
  172.0 2.6 copy-start.12
  172.0 2.8 slice-start
  173.3 289.4 %all-reduce.7.cloned.1.call-start = ((), (), s32[]{:S(2)}) async-start(), calls=%async_computation.1 | async-start | bytes 3735552 | tf_op jit(solution)/shard_map/psum | solution.py:183
  174.6 0.8 copy-start.35
  174.6 68.7 %copy-start.16 = (bf16[144,192]{1,0:T(8,128)(2,1)S(1)}, bf16[144,192]{1,0:T(8,128)(2,1)}, u32[]{:S(2)}) copy-start(bf16[144,192]{1,0:T(8,128)(2,1)} %copy-done.15) | copy-start | bytes 165892
  175.0 70.3 %collective-permute-start.6 = (bf16[4,6,6,192]{3,2,1,0:T(8,128)(2,1)S(1)}, bf16[4,6,6,192]{3,2,1,0:T(8,128)(2,1)S(1)}, u32[]{:S(2)}, u32[]{:S(2)}) collective-permute-start(bf16[4,6,6,192]{3,2,1,0:T(8,128)(2,1)S(1)} %pad_maximum_fusion.7), channel_id=1, source_target_pairs={{0,8},{8,16},{16,24},{24,32},{32,40},{40,48},{48,56},{56,64},{64,7... | collective-permute-start | bytes 165896 | tf_op jit(solution)/shard_map/ppermute | solution.py:12
  244.4 6.9 %collective-permute-start.3 = (bf16[4,3,24,192]{3,2,1,0:T(8,128)(2,1)S(1)}, bf16[4,3,24,192]{3,2,1,0:T(8,128)(2,1)S(1)}, u32[]{:S(2)}, u32[]{:S(2)}) collective-permute-start(bf16[4,3,24,192]{3,2,1,0:T(8,128)(2,1)S(1)} %get-tuple-element.34), channel_id=1, source_target_pairs={{0,1},{1,2},{2,3},{3,4},{4,5},{5,6},{6,7},{7,0},{8,9},{9,10},{10,1... | collective-permute-start | bytes 331784 | tf_op jit(solution)/shard_map/ppermute | solution.py:12
  245.4 9.1 %collective-permute-start.7 = (bf16[4,3,24,192]{3,2,1,0:T(8,128)(2,1)S(1)}, bf16[4,3,24,192]{3,2,1,0:T(8,128)(2,1)S(1)}, u32[]{:S(2)}, u32[]{:S(2)}) collective-permute-start(bf16[4,3,24,192]{3,2,1,0:T(8,128)(2,1)S(1)} %get-tuple-element.30), channel_id=1, source_target_pairs={{0,1},{1,2},{2,3},{3,4},{4,5},{5,6},{6,7},{7,0},{8,9},{9,10},{10,1... | collective-permute-start | bytes 331784 | tf_op jit(solution)/shard_map/ppermute | solution.py:12
  462.8 5.2 %copy-start.18 = (f32[192,768]{1,0:T(8,128)S(1)}, f32[192,768]{1,0:T(8,128)}, u32[]{:S(2)}) copy-start(f32[192,768]{1,0:T(8,128)} %get-tuple-element.57) | copy-start | bytes 1769476
  462.8 6.0 %copy-start.17 = (f32[768,192]{0,1:T(8,128)S(1)}, f32[768,192]{0,1:T(8,128)}, u32[]{:S(2)}) copy-start(f32[768,192]{0,1:T(8,128)} %get-tuple-element.58) | copy-start | bytes 1769476
  462.8 6.8 %copy-start.1 = (bf16[192,768]{1,0:T(8,128)(2,1)S(1)}, bf16[192,768]{1,0:T(8,128)(2,1)}, u32[]{:S(2)}) copy-start(bf16[192,768]{1,0:T(8,128)(2,1)} %param.16) | copy-start | bytes 884740
Sparse Core Ops, SparseCore 0:
  173.5 129.3 all-reduce.4
  310.4 152.3 all-reduce.6
where the time goes:
time: 486 us; the launch traced here: 477 us
  waiting for transfers between devices  216 us (44%)
  local copies, waits for them, and re-layouts  104 us (21%)
  blocking collectives  67.9 us (14%)
  matrix products  49 us (10%)
  between operations  15.1 us (3%)
  starting transfers between devices  13.1 us (3%)
  other arithmetic  11.6 us (2%)
    psum x1, waiting for transfers between devices, local(): lax.psum((g_gain_one, g_w_qkv, g_w_proj, g_gain_two, g_w_in, g_w_out), ('...  160 us
    psum x1, blocking collectives, local(): lax.psum((g_gain_one, g_w_qkv, g_w_proj, g_gain_two, g_w_in, g_w_out), ('...  67.9 us
    psum x1, waiting for transfers between devices, local(): table_total = lax.psum(g_table, 'lon')  47.6 us
    another operation x5, local copies, waits for them, and re-layouts  31.8 us
    add x2, local copies, waits for them, and re-layouts, block_pass(): scores = jnp.where(same_region, scores + pos_bias, -1000000000.0)  30.8 us
    ppermute x8, starting transfers between devices, shifted(): return lax.ppermute(value, axis, pairs)  13 us
    dot_general x1, matrix products, block_pass(): jnp.einsum('rlhacxbdy,oxy->rlhabcdo', d_bias, spread_table, precision=lax...  12.6 us
    unnamed x80, local copies, waits for them, and re-layouts  12.3 us
  transfers between devices with their start and end apart: 10, of which 4 were waited for; matrix products, arithmetic and copies ran while one was open for 23% of the time, Pallas kernels for 0%

commit v1 on v0

v1 whole, which is shorter than its diff:
```python
import functools

import jax
import jax.numpy as jnp
import numpy as np
from jax import lax
from jax.experimental import pallas as pl
from jax.experimental.pallas import tpu as pltpu
from jax.sharding import PartitionSpec as P

HEADS = 6
C = 192
FFH = 768
TOK = 144
WIN = 4
ROWS = WIN * TOK
STACK = HEADS * TOK
POS = 3312
SEG = 138
PACK = 2048
TABLE = 256
MESH = pl.DeviceIdType.MESH
F32 = jnp.float32
BF16 = jnp.bfloat16


def placement_in():
    out = np.zeros((TOK, 240), np.float32)
    for half in range(2):
        for lat in range(6):
            for col in range(12):
                lon = half * 12 + col + 6
                source = lat * 24 + lon if lon < 24 else 144 + lat * 16 + lon - 24
                out[half * 72 + lat * 12 + col, source] = 1
    return out


def placement_out():
    out = np.zeros((240, TOK), np.float32)
    for lat in range(6):
        for col in range(24):
            source = col // 12 * 72 + lat * 12 + col % 12
            out[lat * 24 + col, source] = 1
            if col >= 18:
                out[144 + lat * 16 + col - 18, source] = 1
    return out


def placement_end():
    out = np.zeros((TOK, 240), np.float32)
    for lat in range(6):
        for lon in range(24):
            source = lat * 24 + lon - 6 if lon >= 6 else 144 + lat * 16 + lon
            out[lat * 24 + lon, source] = 1
    return out


def spread_matrix():
    out = np.zeros((512, 256), np.float32)
    for level in range(2):
        for lat in range(6):
            for col in range(12):
                out[level * 256 + lat * 23 + 11 - col, level * 72 + lat * 12 + col] = 1
    return out


def region_masks():
    ids = np.arange(TOK)
    level, lat = ids // 72, ids // 12 % 6 >= 3
    out = np.zeros((2, TOK, TOK), np.float32)
    out[0] = level[:, None] != level[None, :]
    out[1] = lat[:, None] != lat[None, :]
    return out


def head_masks():
    out = np.zeros((8, C), np.float32)
    for head in range(HEADS):
        out[head, head * 32 : head * 32 + 32] = 1
    return out


def mm(left, right):
    return lax.dot_general(left, right, (((1,), (0,)), ((), ())), preferred_element_type=F32)


def mm_nt(left, right):
    return lax.dot_general(left, right, (((1,), (1,)), ((), ())), preferred_element_type=F32)


def mm_tn(left, right):
    return lax.dot_general(left, right, (((0,), (0,)), ((), ())), preferred_element_type=F32)


def norm(values):
    center = values - jnp.mean(values, axis=-1, keepdims=True)
    spread = jnp.mean(center * center, axis=-1, keepdims=True)
    inverse = lax.rsqrt(spread + 1e-05)
    return center * inverse, inverse


def norm_grad(d_normed, gain, unit, inverse):
    d_unit = d_normed * gain
    mean_one = jnp.mean(d_unit, axis=-1, keepdims=True)
    mean_two = jnp.mean(d_unit * unit, axis=-1, keepdims=True)
    return inverse * (d_unit - mean_one - unit * mean_two)


def split_heads(value, heads):
    return jnp.concatenate([value * heads[h : h + 1, :] for h in range(HEADS)], axis=0)


def join_heads(stacked, heads):
    total = stacked[0:TOK, :] * heads[0:1, :]
    for h in range(1, HEADS):
        total = total + stacked[h * TOK : (h + 1) * TOK, :] * heads[h : h + 1, :]
    return total


def segment(cell, other):
    return ((2 * (cell // 6) + other) * 36 + 6 * (cell % 6)) * 23


def expand_bias(bias_ref, spread_ref, masks_ref, parts, flat, stage, bias, last):
    flat[...] = jnp.zeros_like(flat)
    for lev in range(2):
        flat[lev * 8 : lev * 8 + HEADS, 0:POS] = bias_ref[0, lev]
    for lev in range(2):
        for cell in range(12):
            for other in range(2):
                start = segment(cell, other)
                for half in range(2):
                    parts[2 * other + half, pl.ds(lev * 72 + cell, HEADS, stride=12), :] = flat[
                        lev * 8 : lev * 8 + HEADS, start + half * 128 : start + half * 128 + 128
                    ]
    for step in range(12):
        total = None
        for other in range(2):
            value = jnp.concatenate([parts[2 * other], parts[2 * other + 1]], axis=1)
            if step:
                value = pltpu.roll(value, 256 - step, 1)
            matrix = spread_ref[other * 256 : (other + 1) * 256, :]
            for _ in range(3):
                part = value.astype(BF16)
                value = value - part.astype(F32)
                term = mm(part, matrix)
                total = term if total is None else total + term
        for lev in range(2):
            for half in range(2):
                stage[lev, half, pl.ds(step, 72, stride=12), :] = total[
                    lev * 72 : (lev + 1) * 72, half * 128 : half * 128 + 128
                ]
    for lev in range(2):
        closed = masks_ref[1] * last
        if lev == 1:
            closed = closed + masks_ref[0]
        for h in range(HEADS):
            rows = slice(h * TOK, (h + 1) * TOK)
            value = jnp.concatenate([stage[lev, 0, rows, :], stage[lev, 1, rows, 0:16]], axis=1)
            bias[lev, rows, :] = jnp.where(closed > 0.5, -1000000000.0, value)


def reduce_table(d_bias, spread_ref, parts, flat, table):
    sums = [None, None]
    for step in range(12):
        value = jnp.concatenate(
            [
                jnp.concatenate(
                    [d_bias[lev, half, pl.ds(step, 72, stride=12), :] for half in range(2)], axis=1
                )
                for lev in range(2)
            ],
            axis=0,
        )
        high = value.astype(BF16)
        low = (value - high.astype(F32)).astype(BF16)
        for other in range(2):
            matrix = spread_ref[other * 256 : (other + 1) * 256, :]
            term = mm_nt(high, matrix) + mm_nt(low, matrix)
            if step:
                sums[other] = sums[other] + pltpu.roll(term, step, 1)
            else:
                sums[other] = term
    for other in range(2):
        for half in range(2):
            parts[2 * other + half] = sums[other][:, half * 128 : half * 128 + 128]
    flat[...] = jnp.zeros_like(flat)
    for lev in range(2):
        for cell in range(12):
            for other in range(2):
                start = segment(cell, other)
                rows = pl.ds(lev * 72 + cell, HEADS, stride=12)
                flat[lev * 8 : lev * 8 + HEADS, start : start + 128] = parts[2 * other, rows, :]
                flat[lev * 8 : lev * 8 + HEADS, start + 128 : start + SEG] = parts[
                    2 * other + 1, rows, :
                ][:, 0 : SEG - 128]
    for part in range(16):
        table[part * 16 : (part + 1) * 16, :] = flat[:, part * 256 : (part + 1) * 256]


def gather_level(own, below, east, corner, matrix, lev):
    source = (lev + 1) % 4
    parts = [
        own[source, 3:6].astype(F32).reshape(72, C),
        below[source].astype(F32).reshape(72, C),
        east[source].astype(F32).reshape(48, C),
        corner[source].astype(F32).reshape(48, C),
    ]
    return mm(matrix, jnp.concatenate(parts, axis=0).astype(BF16))


def gather_all(own, halos, matrix, out):
    below, east, corner = halos
    for lev in range(4):
        rows = gather_level(own, below, east, corner, matrix, lev)
        for half in range(2):
            start = ((lev // 2) * 2 + half) * TOK + (lev % 2) * 72
            out[start : start + 72, :] = rows[half * 72 : (half + 1) * 72, :].astype(out.dtype)


def scatter_all(value, matrix, full, side):
    for lev in range(4):
        parts = []
        for half in range(2):
            start = ((lev // 2) * 2 + half) * TOK + (lev % 2) * 72
            parts.append(value[start : start + 72, :].astype(F32))
        rows = mm(matrix, jnp.concatenate(parts, axis=0).astype(BF16))
        full[lev] = rows[0:144].reshape(6, 24, C).astype(BF16)
        side[lev] = rows[144:240].reshape(6, 16, C).astype(BF16)


def block_kernel(
    n_k,
    n_l,
    fields,
    cotangent,
    bias_ref,
    gain_one,
    w_qkv,
    w_proj,
    gain_two,
    w_in,
    w_out,
    place_in,
    place_out,
    spread_ref,
    masks_ref,
    heads_ref,
    gathered,
    full_out,
    below_out,
    east_out,
    corner_out,
    below,
    east,
    corner,
    side,
    x_ref,
    cot_ref,
    n1_ref,
    q_ref,
    k_ref,
    v_ref,
    bias,
    probs,
    att_ref,
    act_ref,
    dpre_ref,
    n2_ref,
    dbb_ref,
    dbranch_ref,
    datt_ref,
    out_ref,
    dq_ref,
    dk_ref,
    dv_ref,
    d_bias,
    pack,
    parts,
    stage,
    flat,
    table,
    send_pair,
    recv_pair,
    send_lon,
    recv_lon,
    send_lat,
    recv_lat,
    total,
    in_send,
    in_recv,
    out_send,
    out_recv,
    pair_send,
    pair_recv,
    lon_send,
    lon_recv,
    lat_send,
    lat_recv,
    glat_send,
    glat_recv,
    glon_send,
    glon_recv,
    gpair_send,
    gpair_recv,
):
    n_lon = 2 * n_k
    chunk = PACK // n_lon
    rest = TABLE // n_lon
    piece = chunk // n_l
    lon, lat = lax.axis_index("lon"), lax.axis_index("lat")
    core, k = lax.rem(lon, 2), lon // 2
    other = 1 - core

    def at(d_lon, d_lat):
        return (lax.rem(lon + d_lon + n_lon, n_lon), lax.rem(lat + d_lat + n_l, n_l))

    def in_lon8(d):
        return (2 * lax.rem(k + d, n_k) + core, lat)

    partner = (2 * k + other, lat)
    far_lon = lax.rem(lon + 2 * core - 1 + n_lon, n_lon)

    friends = [partner, (far_lon, lat), at(1, 1), at(-1, -1)]
    friends += [in_lon8(d) for d in range(1, n_k)]
    friends += [at(0, d) for d in range(1, n_l)]
    barrier = pltpu.get_barrier_semaphore()
    for friend in friends:
        pl.semaphore_signal(barrier, inc=1, device_id=friend, device_id_type=MESH)
    pl.semaphore_wait(barrier, len(friends))

    def copy(source, target, send, recv, device):
        return pltpu.make_async_remote_copy(
            src_ref=source,
            dst_ref=target,
            send_sem=send,
            recv_sem=recv,
            device_id=device,
            device_id_type=MESH,
        )

    in_copies = []
    for i, source in enumerate((fields, cotangent)):
        in_copies.append(
            [
                copy(source.at[:, 0:3], below.at[i], in_send.at[i, 0], in_recv.at[i, 0], at(0, -1)),
                copy(
                    source.at[:, 3:6, 0:16],
                    east.at[i],
                    in_send.at[i, 1],
                    in_recv.at[i, 1],
                    at(-1, 0),
                ),
                copy(
                    source.at[:, 0:3, 0:16],
                    corner.at[i],
                    in_send.at[i, 2],
                    in_recv.at[i, 2],
                    at(-1, -1),
                ),
            ]
        )
        for c in in_copies[i]:
            c.start()

    def send_out(i):
        copies = [
            copy(
                full_out.at[i, :, 3:6],
                below_out.at[i],
                out_send.at[i, 0],
                out_recv.at[i, 0],
                at(0, 1),
            ),
            copy(side.at[i, :, 0:3], east_out.at[i], out_send.at[i, 1], out_recv.at[i, 1], at(1, 0)),
            copy(
                side.at[i, :, 3:6],
                corner_out.at[i],
                out_send.at[i, 2],
                out_recv.at[i, 2],
                at(1, 1),
            ),
        ]
        for c in copies:
            c.start()
        return copies

    last = (lat == n_l - 1).astype(F32)
    expand_bias(bias_ref, spread_ref, masks_ref, parts, flat, stage, bias, last)

    heads = heads_ref[...]
    heads32 = heads.astype(F32)
    scale = 32**-0.5
    gain1 = gain_one[...]
    gain2 = gain_two[...]

    for c in in_copies[0]:
        c.wait_recv()
    gather_all(fields, (below.at[0], east.at[0], corner.at[0]), place_in[...], x_ref)
    unit, _ = norm(x_ref[...])
    n1 = (unit * gain1).astype(BF16)
    n1_ref[...] = n1
    for i, ref in enumerate((q_ref, k_ref, v_ref)):
        ref[...] = mm(n1, w_qkv[:, i * C : (i + 1) * C]).astype(BF16)

    def attend(w, carry):
        rows = pl.ds(pl.multiple_of(w * TOK, TOK), TOK)
        stacked = split_heads(q_ref[rows, :], heads)
        scores = mm_nt(stacked, k_ref[rows, :]) * scale + bias[w // 2]
        top = jnp.max(scores, axis=-1, keepdims=True)
        exps = jnp.exp(scores - top)
        prob = exps * (1.0 / jnp.sum(exps, axis=-1, keepdims=True))
        probs[w] = prob
        mixed = mm(prob.astype(BF16), v_ref[rows, :])
        att_ref[rows, :] = join_heads(mixed, heads32).astype(BF16)
        return carry

    lax.fori_loop(0, WIN, attend, 0)

    for c in in_copies[1]:
        c.wait_recv()
    gather_all(cotangent, (below.at[1], east.at[1], corner.at[1]), place_in[...], cot_ref)

    half = ROWS // 2

    def feed(i, gain_sum):
        rows = pl.ds(pl.multiple_of(i * half, half), half)
        branch = x_ref[rows, :] + mm(att_ref[rows, :], w_proj[...])
        unit, inverse = norm(branch)
        n2 = (unit * gain2).astype(BF16)
        n2_ref[rows, :] = n2
        pre = mm(n2, w_in[...])
        cdf = 0.5 + 0.5 * lax.erf(pre * (0.5**0.5))
        slope = cdf + pre * (jnp.exp(-0.5 * pre * pre) * ((2.0 * np.pi) ** -0.5))
        act = (pre * cdf).astype(BF16)
        act_ref[rows, :] = act
        out_ref[rows, :] = branch + mm(act, w_out[...])
        cot = cot_ref[rows, :]
        d_pre = (slope * mm_nt(cot, w_out[...])).astype(BF16)
        dpre_ref[rows, :] = d_pre
        d_normed = mm_nt(d_pre, w_in[...])
        d_branch = cot.astype(F32) + norm_grad(d_normed, gain2, unit, inverse)
        dbranch_ref[rows, :] = d_branch
        dbb = d_branch.astype(BF16)
        dbb_ref[rows, :] = dbb
        datt_ref[rows, :] = mm_nt(dbb, w_proj[...]).astype(BF16)
        return gain_sum + jnp.sum(d_normed * unit, axis=0, keepdims=True)

    gain_sum2 = lax.fori_loop(0, 2, feed, jnp.zeros((1, C), F32))
    scatter_all(out_ref, place_out[...], full_out.at[0], side.at[0])
    out_copies = send_out(0)

    pack[1152:PACK, 128:256] = jnp.zeros((PACK - 1152, 128), F32)
    pack[1920:PACK, 0:128] = jnp.zeros((PACK - 1920, 128), F32)
    pack[1928:1929, 0:C] = gain_sum2
    for i in range(3):
        cols = slice(i * 256, (i + 1) * 256)
        pack[i * C : (i + 1) * C, :] = mm_tn(cot_ref[...], act_ref[:, cols])
        pack[576 + i * C : 576 + (i + 1) * C, :] = mm_tn(n2_ref[...], dpre_ref[:, cols])
    pack[1152 : 1152 + C, 0:C] = mm_tn(att_ref[...], dbb_ref[...])

    d_bias[...] = jnp.zeros_like(d_bias)

    def attend_back(w, carry):
        rows = pl.ds(pl.multiple_of(w * TOK, TOK), TOK)
        prob = probs[w]
        d_stacked = split_heads(datt_ref[rows, :], heads)
        d_prob = mm_nt(d_stacked, v_ref[rows, :])
        d_score = prob * (d_prob - jnp.sum(d_prob * prob, axis=-1, keepdims=True))
        d_bias[w // 2, 0] += d_score[:, 0:128]
        d_bias[w // 2, 1, :, 0:16] += d_score[:, 128:144]
        d_score_b = d_score.astype(BF16)
        dv_ref[rows, :] = mm_tn(prob.astype(BF16), d_stacked).astype(BF16)
        dq_ref[rows, :] = (join_heads(mm(d_score_b, k_ref[rows, :]), heads32) * scale).astype(BF16)
        stacked = split_heads(q_ref[rows, :], heads)
        dk_ref[rows, :] = (mm_tn(d_score_b, stacked) * scale).astype(BF16)
        return carry

    lax.fori_loop(0, WIN, attend_back, 0)

    d_normed = None
    for i, ref in enumerate((dq_ref, dk_ref, dv_ref)):
        pack[1344 + i * C : 1344 + (i + 1) * C, 0:C] = mm_tn(n1_ref[...], ref[...])
        term = mm_nt(ref[...], w_qkv[:, i * C : (i + 1) * C])
        d_normed = term if d_normed is None else d_normed + term
    unit, inverse = norm(x_ref[...])
    pack[1920:1921, 0:C] = jnp.sum(d_normed * unit, axis=0, keepdims=True)
    out_ref[...] = dbranch_ref[...] + norm_grad(d_normed, gain1, unit, inverse)
    scatter_all(out_ref, place_out[...], full_out.at[1], side.at[1])
    out_copies += send_out(1)
    reduce_table(d_bias, spread_ref, parts, flat, table)

    def pack_rows(c, kk):
        start = pl.multiple_of((2 * kk + c) * chunk, chunk)
        return pack[pl.ds(start, chunk), :]

    def table_rows(c, kk):
        start = pl.multiple_of((2 * kk + c) * rest, rest)
        return table[pl.ds(start, rest), :]

    sends = []

    def start(c):
        c.start()
        sends.append(c)
        return c

    pair = []
    for d in range(1, n_k + 1):
        kk = lax.rem(k + d, n_k)
        send_pair[d - 1, 0:chunk, :] = pack_rows(other, kk).astype(BF16)
        send_pair[d - 1, chunk : chunk + rest, :] = table_rows(other, kk).astype(BF16)
        pair.append(
            start(
                copy(
                    send_pair.at[d - 1],
                    recv_pair.at[d - 1],
                    pair_send.at[d - 1],
                    pair_recv.at[d - 1],
                    partner,
                )
            )
        )
    along_lon = []
    for d in range(1, n_k + 1):
        kk = lax.rem(k + d, n_k)
        pair[d - 1].wait_recv()
        top = pack_rows(core, kk) + recv_pair[d - 1, 0:chunk, :].astype(F32)
        end = table_rows(core, kk) + recv_pair[d - 1, chunk : chunk + rest, :].astype(F32)
        if d < n_k:
            send_lon[d - 1, 0:chunk, :] = top.astype(BF16)
            send_lon[d - 1, chunk : chunk + rest, :] = end.astype(BF16)
            along_lon.append(
                start(
                    copy(
                        send_lon.at[d - 1],
                        recv_lon.at[d - 1],
                        lon_send.at[d - 1],
                        lon_recv.at[d - 1],
                        in_lon8(d),
                    )
                )
            )
        else:
            total[0:chunk, :] = top
            total[chunk : chunk + rest, :] = end
    for d in range(1, n_k):
        along_lon[d - 1].wait_recv()
        total[...] += recv_lon[d - 1].astype(F32)

    def piece_at(d):
        return pl.ds(pl.multiple_of(lax.rem(lat + d + n_l, n_l) * piece, piece), piece)

    along_lat = []
    for d in range(1, n_l):
        send_lat[d - 1] = total[piece_at(d), :].astype(BF16)
        along_lat.append(
            start(
                copy(
                    send_lat.at[d - 1],
                    recv_lat.at[d - 1],
                    lat_send.at[d - 1],
                    lat_recv.at[d - 1],
                    at(0, d),
                )
            )
        )
    final = total[piece_at(0), :]
    for d in range(1, n_l):
        along_lat[d - 1].wait_recv()
        final = final + recv_lat[d - 1].astype(F32)
    gathered[core, k, piece_at(0), :] = final.astype(BF16)
    gathered[core, k, chunk : chunk + rest, :] = total[chunk : chunk + rest, :].astype(BF16)

    for d in range(1, n_l):
        mine = gathered.at[core, k, piece_at(0), :]
        start(copy(mine, mine, glat_send.at[d - 1], glat_recv.at[d - 1], at(0, d)))
    for d in range(1, n_l):
        theirs = gathered.at[core, k, piece_at(-d), :]
        copy(theirs, theirs, glat_send.at[d - 1], glat_recv.at[d - 1], partner).wait_recv()
    mine = gathered.at[core, k]
    for d in range(1, n_k):
        start(copy(mine, mine, glon_send.at[d - 1], glon_recv.at[d - 1], in_lon8(d)))
    start(copy(mine, mine, gpair_send.at[0], gpair_recv.at[0], partner))
    for d in range(1, n_k):
        theirs = gathered.at[core, lax.rem(k - d + n_k, n_k)]
        copy(theirs, theirs, glon_send.at[d - 1], glon_recv.at[d - 1], partner).wait_recv()
        start(copy(theirs, theirs, gpair_send.at[d], gpair_recv.at[d], partner))
    for d in range(n_k):
        theirs = gathered.at[other, lax.rem(k - d + n_k, n_k)]
        copy(theirs, theirs, gpair_send.at[d], gpair_recv.at[d], partner).wait_recv()

    for c in out_copies:
        c.wait_recv()
    for c in in_copies[0] + in_copies[1] + out_copies + sends:
        c.wait_send()


def finish_kernel(
    n_k,
    gathered,
    full_out,
    below_out,
    east_out,
    corner_out,
    place_end,
    block_out,
    grad_fields,
    g_gain_one,
    g_w_qkv,
    g_table,
    g_w_proj,
    g_gain_two,
    g_w_in,
    g_w_out,
    weights,
):
    n_lon = 2 * n_k
    chunk = PACK // n_lon
    rest = TABLE // n_lon
    for i, ref in enumerate((block_out, grad_fields)):
        for lev in range(4):
            parts = [
                below_out[i, lev].astype(F32).reshape(72, C),
                full_out[i, lev, 0:3].astype(F32).reshape(72, C),
                corner_out[i, lev].astype(F32).reshape(48, C),
                east_out[i, lev].astype(F32).reshape(48, C),
            ]
            rows = mm(place_end[...], jnp.concatenate(parts, axis=0).astype(BF16))
            ref[(lev + 1) % 4] = rows.reshape(6, 24, C).astype(BF16)
    for part in range(n_lon):
        weights[part * chunk : (part + 1) * chunk, :] = gathered[
            part % 2, part // 2, 0:chunk, :
        ].astype(F32)
    for i in range(3):
        cols = slice(i * 256, (i + 1) * 256)
        g_w_out[cols, :] = weights[i * C : (i + 1) * C, :].T
        g_w_in[:, cols] = weights[576 + i * C : 576 + (i + 1) * C, :]
        g_w_qkv[:, i * C : (i + 1) * C] = weights[1344 + i * C : 1344 + (i + 1) * C, 0:C]
    g_w_proj[...] = weights[1152 : 1152 + C, 0:C]
    g_gain_one[...] = weights[1920:1921, 0:C]
    g_gain_two[...] = weights[1928:1929, 0:C]
    for part in range(13):
        width = min(256, POS - part * 256)
        place, offset = divmod(part * 16, rest)
        value = gathered[place % 2, place // 2, chunk + offset : chunk + offset + 16, :].astype(F32)
        for lev in range(2):
            g_table[0, lev, :, part * 256 : part * 256 + width] = value[
                lev * 8 : lev * 8 + HEADS, 0:width
            ]


def local(n_k, n_l, fields, cotangent, bias_table, gain_one, w_qkv, w_proj, gain_two, w_in, w_out):
    n_lon = 2 * n_k
    chunk = PACK // n_lon
    rest = TABLE // n_lon
    piece = chunk // n_l
    sds = jax.ShapeDtypeStruct
    vmem = pltpu.VMEM
    dma = pltpu.SemaphoreType.DMA
    whole = pl.BlockSpec(memory_space=pltpu.VMEM)
    moved = (
        sds((2, n_k, chunk + rest, 256), BF16),
        sds((2, 4, 6, 24, C), BF16),
        sds((2, 4, 3, 24, C), BF16),
        sds((2, 4, 3, 16, C), BF16),
        sds((2, 4, 3, 16, C), BF16),
    )
    results = pl.pallas_call(
        functools.partial(block_kernel, n_k, n_l),
        out_shape=moved,
        in_specs=[whole] * 14,
        out_specs=[whole] * 5,
        scratch_shapes=[
            vmem((2, 4, 3, 24, C), BF16),
            vmem((2, 4, 3, 16, C), BF16),
            vmem((2, 4, 3, 16, C), BF16),
            vmem((2, 4, 6, 16, C), BF16),
            vmem((ROWS, C), F32),
            vmem((ROWS, C), BF16),
            vmem((ROWS, C), BF16),
            vmem((ROWS, C), BF16),
            vmem((ROWS, C), BF16),
            vmem((ROWS, C), BF16),
            vmem((2, STACK, TOK), F32),
            vmem((WIN, STACK, TOK), F32),
            vmem((ROWS, C), BF16),
            vmem((ROWS, FFH), BF16),
            vmem((ROWS, FFH), BF16),
            vmem((ROWS, C), BF16),
            vmem((ROWS, C), BF16),
            vmem((ROWS, C), F32),
            vmem((ROWS, C), BF16),
            vmem((ROWS, C), F32),
            vmem((ROWS, C), BF16),
            vmem((ROWS, C), BF16),
            vmem((ROWS, C), BF16),
            vmem((2, 2, STACK, 128), F32),
            vmem((PACK, 256), F32),
            vmem((4, TOK, 128), F32),
            vmem((2, 2, STACK, 128), F32),
            vmem((16, 4096), F32),
            vmem((TABLE, 256), F32),
            vmem((n_k, chunk + rest, 256), BF16),
            vmem((n_k, chunk + rest, 256), BF16),
            vmem((n_k - 1, chunk + rest, 256), BF16),
            vmem((n_k - 1, chunk + rest, 256), BF16),
            vmem((n_l - 1, piece, 256), BF16),
            vmem((n_l - 1, piece, 256), BF16),
            vmem((chunk + rest, 256), F32),
            dma((2, 3)),
            dma((2, 3)),
            dma((2, 3)),
            dma((2, 3)),
            dma((n_k,)),
            dma((n_k,)),
            dma((n_k - 1,)),
            dma((n_k - 1,)),
            dma((n_l - 1,)),
            dma((n_l - 1,)),
            dma((n_l - 1,)),
            dma((n_l - 1,)),
            dma((n_k - 1,)),
            dma((n_k - 1,)),
            dma((n_k,)),
            dma((n_k,)),
        ],
        compiler_params=pltpu.CompilerParams(
            collective_id=0, has_side_effects=True, vmem_limit_bytes=56 * 1024 * 1024
        ),
        name="block",
    )(
        fields,
        cotangent,
        bias_table,
        gain_one.reshape(1, C),
        w_qkv,
        w_proj,
        gain_two.reshape(1, C),
        w_in,
        w_out,
        jnp.asarray(placement_in(), BF16),
        jnp.asarray(placement_out(), BF16),
        jnp.asarray(spread_matrix(), BF16),
        jnp.asarray(region_masks(), F32),
        jnp.asarray(head_masks(), BF16),
    )
    outs = pl.pallas_call(
        functools.partial(finish_kernel, n_k),
        out_shape=(
            sds((4, 6, 24, C), BF16),
            sds((4, 6, 24, C), BF16),
            sds((1, C), F32),
            sds((C, 3 * C), F32),
            sds((1, 2, HEADS, POS), F32),
            sds((C, C), F32),
            sds((1, C), F32),
            sds((C, FFH), F32),
            sds((FFH, C), F32),
        ),
        in_specs=[whole] * 6,
        out_specs=[whole] * 9,
        scratch_shapes=[vmem((PACK, 256), F32)],
        compiler_params=pltpu.CompilerParams(vmem_limit_bytes=48 * 1024 * 1024),
        name="finish",
    )(*results, jnp.asarray(placement_end(), BF16))
    outs = list(outs)
    outs[2] = outs[2].reshape(C)
    outs[6] = outs[6].reshape(C)
    return tuple(outs)


def solution(mesh):
    n_k, n_l = mesh.shape["lon"] // 2, mesh.shape["lat"]
    placed = (
        P(None, "lat", "lon", None),
        P(None, "lat", "lon", None),
        P("lat", None, None, None),
    ) + (P(),) * 6
    return jax.shard_map(
        functools.partial(local, n_k, n_l),
        mesh=mesh,
        in_specs=placed,
        out_specs=(
            P(None, "lat", "lon", None),
            P(None, "lat", "lon", None),
            P(),
            P(),
            P("lat", None, None, None),
            P(),
            P(),
            P(),
            P(),
        ),
        check_vma=False,
    )
```

time: 486 us -> 80.4 us (0.17); the launches traced: 477 us -> 80 us
  waiting for transfers between devices: 216 us -> 0 us
  local copies, waits for them, and re-layouts: 104 us -> 10.5 us
  Pallas kernels: 0 us -> 68.9 us
  blocking collectives: 67.9 us -> 0 us
  matrix products: 49 us -> 0 us
  between operations: 15.1 us -> 0.67 us
  starting transfers between devices: 13.1 us -> 0 us
  other arithmetic: 11.6 us -> 0 us
    psum x2 -> x0, waiting for transfers between devices: 208 us -> none  [the longest x1 160 us: local(): lax.psum((g_gain_one, g_w_qkv, g_w_proj, g_gain_two, g_w_in, g_w_out), ('...]
    pallas_call x0 -> x2, Pallas kernels: none -> 68.9 us  [the longest x1 67.4 us: local(): pl.pallas_call(functools.partial(block_kernel, n_k, n_l), out_shape=moved...]
    psum x1 -> x0, blocking collectives: 67.9 us -> none  [local(): lax.psum((g_gain_one, g_w_qkv, g_w_proj, g_gain_two, g_w_in, g_w_out), ('...]
    another operation x13 -> x0, local copies, waits for them, and re-layouts: 49 us -> none
    dot_general x19 -> x0, matrix products: 44 us -> none  [the longest x1 12.6 us: block_pass(): jnp.einsum('rlhacxbdy,oxy->rlhabcdo', d_bias, spread_table, precision=lax...]
    add x3 -> x0, local copies, waits for them, and re-layouts: 30.9 us -> none  [the longest x2 30.8 us: block_pass(): scores = jnp.where(same_region, scores + pos_bias, -1000000000.0)]
    ppermute x8 -> x0, starting transfers between devices: 13 us -> none  [shifted(): return lax.ppermute(value, axis, pairs)]
    ppermute x8 -> x0, waiting for transfers between devices: 8.21 us -> none  [shifted(): return lax.ppermute(value, axis, pairs)]
  transfers between devices with their start and end apart: 10 -> 0, of which waited for: 4 -> 0; matrix products, arithmetic and copies ran while one was open for 23% -> 0% of each run, Pallas kernels for 0% -> 0%
where the time goes in v1:
time: 80.4 us; the launch traced here: 80 us
  Pallas kernels  68.9 us (86%)
  local copies, waits for them, and re-layouts  10.5 us (13%)
    pallas_call x1, Pallas kernels, local(): pl.pallas_call(functools.partial(block_kernel, n_k, n_l), out_shape=moved...  67.4 us
    unnamed x16, local copies, waits for them, and re-layouts  10.5 us

profile of v1, /device:TPU:1, one launch (start us, length us, event | category | flops | bytes accessed | tf_op | source)
XLA Modules:
  0.0 80.0 jit_solution(9679952801128136247)
XLA Ops:
  0.6 1.6 %copy.24.bias_ref = f32[1,2,6,3312]{3,2,1,0:T(8,128)} copy(f32[1,2,6,3312]{3,1,2,0:T(2,128)} %param.17) | data formatting | bytes 317952 | tf_op args[2]
  2.3 1.9 %copy.25.w_out = bf16[768,192]{1,0:T(8,128)(2,1)} copy(bf16[768,192]{0,1:T(8,128)(2,1)} %param.23) | data formatting | bytes 589824 | tf_op args[8]
  4.1 0.0 copy-start.5
  4.1 67.4 %block.1 = (bf16[2,8,144,256]{3,2,1,0:T(8,128)(2,1)}, bf16[2,4,6,24,192]{4,3,2,1,0:T(8,128)(2,1)}, bf16[2,4,3,24,192]{4,3,2,1,0:T(8,128)(2,1)}, bf16[2,4,3,16,19...) custom-call(bf16[4,6,24,192]{3,2,1,0:T(8,128)(2,1)} %fields.1, bf16[4,6,24,192]{3,2,1,0:T(8,128)(2,1)} %cotangent.1, ...), custom_call_target="tpu_custom_call" | custom-call | tf_op jit(solution)/shard_map/block/pallas_call | solution.py:669
  71.5 0.0 copy-done.5
  71.5 0.0 copy-start
  71.6 1.3 %copy-done = bf16[2,8,144,256]{3,2,1,0:T(8,128)(2,1)S(1)} copy-done((bf16[2,8,144,256]{3,2,1,0:T(8,128)(2,1)S(1)}, bf16[2,8,144,256]{3,2,1,0:T(8,128)(2,1)}, u32[]{:S(2)}) %copy-start) | copy-done | bytes 1179672
  72.8 0.0 copy-start.1
  72.8 1.1 %copy-done.1 = bf16[2,4,6,24,192]{4,3,2,1,0:T(8,128)(2,1)S(1)} copy-done((bf16[2,4,6,24,192]{4,3,2,1,0:T(8,128)(2,1)S(1)}, bf16[2,4,6,24,192]{4,3,2,1,0:T(8,128)(2,1)}, u32[]{:S(2)}) %copy-start.1) | copy-done | bytes 442392
  73.9 0.0 copy-start.2
  73.9 1.0 %copy-done.2 = bf16[2,4,3,24,192]{4,3,2,1,0:T(8,128)(2,1)S(1)} copy-done((bf16[2,4,3,24,192]{4,3,2,1,0:T(8,128)(2,1)S(1)}, bf16[2,4,3,24,192]{4,3,2,1,0:T(8,128)(2,1)}, u32[]{:S(2)}) %copy-start.2) | copy-done | bytes 221208
  74.8 0.0 copy-start.3
  74.8 0.9 %copy-done.3 = bf16[2,4,3,16,192]{4,3,2,1,0:T(8,128)(2,1)S(1)} copy-done((bf16[2,4,3,16,192]{4,3,2,1,0:T(8,128)(2,1)S(1)}, bf16[2,4,3,16,192]{4,3,2,1,0:T(8,128)(2,1)}, u32[]{:S(2)}) %copy-start.3) | copy-done | bytes 147480
  75.8 0.0 copy-start.4
  75.8 0.9 %copy-done.4 = bf16[2,4,3,16,192]{4,3,2,1,0:T(8,128)(2,1)S(1)} copy-done((bf16[2,4,3,16,192]{4,3,2,1,0:T(8,128)(2,1)S(1)}, bf16[2,4,3,16,192]{4,3,2,1,0:T(8,128)(2,1)}, u32[]{:S(2)}) %copy-start.4) | copy-done | bytes 147480
  76.7 1.5 %finish.1 = (bf16[4,6,24,192]{3,2,1,0:T(8,128)(2,1)}, bf16[4,6,24,192]{3,2,1,0:T(8,128)(2,1)}, f32[1,192]{1,0:T(1,128)}, f32[192,576]{1,0:T(8,128)}, f32[1,2,6,3...) custom-call(bf16[2,8,144,256]{3,2,1,0:T(8,128)(2,1)S(1)} %copy-done,, ...), custom_call_target="tpu_custom_call" | custom-call | tf_op jit(solution)/shard_map/finish/pallas_call | solution.py:748
  78.2 0.7 copy.26
  78.9 1.1 %copy.27 = f32[768,192]{0,1:T(8,128)} copy(f32[768,192]{1,0:T(8,128)S(1)} %get-tuple-element.45) | data formatting | bytes 1179648
Async XLA Ops:
  4.1 67.4 %copy-start.5 = (bf16[144,240]{1,0:T(8,128)(2,1)S(1)}, bf16[144,240]{1,0:T(8,128)(2,1)}, u32[]{:S(2)}) copy-start(bf16[144,240]{1,0:T(8,128)(2,1)} %constant.17.clone.place_end) | copy-start | bytes 207364
  71.5 1.3 %copy-start = (bf16[2,8,144,256]{3,2,1,0:T(8,128)(2,1)S(1)}, bf16[2,8,144,256]{3,2,1,0:T(8,128)(2,1)}, u32[]{:S(2)}) copy-start(bf16[2,8,144,256]{3,2,1,0:T(8,128)(2,1)} %get-tuple-element.23.gathered) | copy-start | bytes 3538948
  72.8 1.1 %copy-start.1 = (bf16[2,4,6,24,192]{4,3,2,1,0:T(8,128)(2,1)S(1)}, bf16[2,4,6,24,192]{4,3,2,1,0:T(8,128)(2,1)}, u32[]{:S(2)}) copy-start(bf16[2,4,6,24,192]{4,3,2,1,0:T(8,128)(2,1)} %get-tuple-element.24.full_out) | copy-start | bytes 1327108
  73.9 1.0 %copy-start.2 = (bf16[2,4,3,24,192]{4,3,2,1,0:T(8,128)(2,1)S(1)}, bf16[2,4,3,24,192]{4,3,2,1,0:T(8,128)(2,1)}, u32[]{:S(2)}) copy-start(bf16[2,4,3,24,192]{4,3,2,1,0:T(8,128)(2,1)} %get-tuple-element.25.below_out) | copy-start | bytes 663556
  74.8 0.9 %copy-start.3 = (bf16[2,4,3,16,192]{4,3,2,1,0:T(8,128)(2,1)S(1)}, bf16[2,4,3,16,192]{4,3,2,1,0:T(8,128)(2,1)}, u32[]{:S(2)}) copy-start(bf16[2,4,3,16,192]{4,3,2,1,0:T(8,128)(2,1)} %get-tuple-element.26.east_out) | copy-start | bytes 442372
  75.8 0.9 %copy-start.4 = (bf16[2,4,3,16,192]{4,3,2,1,0:T(8,128)(2,1)S(1)}, bf16[2,4,3,16,192]{4,3,2,1,0:T(8,128)(2,1)}, u32[]{:S(2)}) copy-start(bf16[2,4,3,16,192]{4,3,2,1,0:T(8,128)(2,1)} %get-tuple-element.27.corner_out) | copy-start | bytes 442372

commit v2 on v1

v2 whole, which is shorter than its diff:
```python
import functools

import jax
import jax.numpy as jnp
import numpy as np
from jax import lax
from jax.experimental import pallas as pl
from jax.experimental.pallas import tpu as pltpu
from jax.sharding import PartitionSpec as P

HEADS = 6
C = 192
FFH = 768
TOK = 144
WIN = 4
ROWS = WIN * TOK
STACK = HEADS * TOK
POS = 3312
SEG = 138
EARLY = 1536
LATE = 768
TABLE = 256
EDGE = 80
MESH = pl.DeviceIdType.MESH
F32 = jnp.float32
BF16 = jnp.bfloat16


def window_row(lev, lat, col):
    return ((lev // 2) * 2 + col // 12) * TOK + (lev % 2) * 72 + lat * 12 + col % 12


def place_level_in():
    out = np.zeros((TOK, TOK), np.float32)
    for lat in range(6):
        for col in range(18):
            out[col // 12 * 72 + lat * 12 + col % 12, lat * 24 + col + 6] = 1
    return out


def edge_row(lev, lat, col):
    return (0 if lat < 3 else EDGE) + lev * 18 + lat % 3 * 6 + col


def place_edge_in():
    out = np.zeros((4, TOK, 2 * EDGE), np.float32)
    for lev in range(4):
        for lat in range(6):
            for col in range(6):
                out[lev, 72 + lat * 12 + 6 + col, edge_row((lev + 1) % 4, lat, col)] = 1
    return out


def pick_edge_in():
    out = np.zeros((2 * EDGE, ROWS), np.float32)
    for lev in range(4):
        for lat in range(6):
            for col in range(6):
                out[edge_row(lev, (lat + 3) % 6, col), (lev * 6 + lat) * 24 + col] = 1
    return out


def place_level_out():
    out = np.zeros((TOK, TOK), np.float32)
    for lat in range(6):
        for col in range(24):
            out[lat * 24 + col, col // 12 * 72 + lat * 12 + col % 12] = 1
    return out


def pick_edge_out():
    out = np.zeros((2 * EDGE, ROWS), np.float32)
    for lev in range(4):
        for lat in range(6):
            for col in range(6):
                out[edge_row(lev, lat, col), window_row(lev, lat, 18 + col)] = 1
    return out


def place_level_end():
    out = np.zeros((TOK, TOK), np.float32)
    for lat in range(6):
        for lon in range(6, 24):
            out[lat * 24 + lon, lat * 24 + lon - 6] = 1
    return out


def place_edge_end():
    out = np.zeros((4, TOK, 2 * EDGE), np.float32)
    for lev in range(4):
        for lat in range(6):
            for lon in range(6):
                out[lev, lat * 24 + lon, edge_row(lev, (lat + 3) % 6, lon)] = 1
    return out


def spread_matrix():
    out = np.zeros((512, 256), np.float32)
    for level in range(2):
        for lat in range(6):
            for col in range(12):
                out[level * 256 + lat * 23 + 11 - col, level * 72 + lat * 12 + col] = 1
    return out


def region_masks():
    ids = np.arange(TOK)
    level, lat = ids // 72, ids // 12 % 6 >= 3
    out = np.zeros((2, TOK, TOK), np.float32)
    out[0] = level[:, None] != level[None, :]
    out[1] = lat[:, None] != lat[None, :]
    return out


def head_masks():
    out = np.zeros((8, C), np.float32)
    for head in range(HEADS):
        out[head, head * 32 : head * 32 + 32] = 1
    return out


def mm(left, right):
    return lax.dot_general(left, right, (((1,), (0,)), ((), ())), preferred_element_type=F32)


def mm_nt(left, right):
    return lax.dot_general(left, right, (((1,), (1,)), ((), ())), preferred_element_type=F32)


def mm_tn(left, right):
    return lax.dot_general(left, right, (((0,), (0,)), ((), ())), preferred_element_type=F32)


def norm(values):
    center = values - jnp.mean(values, axis=-1, keepdims=True)
    spread = jnp.mean(center * center, axis=-1, keepdims=True)
    inverse = lax.rsqrt(spread + 1e-05)
    return center * inverse, inverse


def norm_grad(d_normed, gain, unit, inverse):
    d_unit = d_normed * gain
    mean_one = jnp.mean(d_unit, axis=-1, keepdims=True)
    mean_two = jnp.mean(d_unit * unit, axis=-1, keepdims=True)
    return inverse * (d_unit - mean_one - unit * mean_two)


def split_heads(value, heads):
    return jnp.concatenate([value * heads[h : h + 1, :] for h in range(HEADS)], axis=0)


def join_heads(stacked, heads):
    total = stacked[0:TOK, :] * heads[0:1, :]
    for h in range(1, HEADS):
        total = total + stacked[h * TOK : (h + 1) * TOK, :] * heads[h : h + 1, :]
    return total


def segment(cell, other):
    return ((2 * (cell // 6) + other) * 36 + 6 * (cell % 6)) * 23


def segment(cell, other):
    return ((2 * (cell // 6) + other) * 36 + 6 * (cell % 6)) * 23


def expand_bias(bias_ref, spread_ref, masks_ref, parts, flat, stage, bias, last):
    flat[...] = jnp.zeros_like(flat)
    for h in range(HEADS):
        flat[2 * h : 2 * h + 2, 0:POS] = bias_ref[0, h]
    for cell in range(12):
        for other in range(2):
            start = segment(cell, other)
            for half in range(2):
                parts[2 * other + half, pl.ds(cell, 12, stride=12), :] = flat[
                    0:12, start + half * 128 : start + half * 128 + 128
                ]
    for step in range(12):
        total = None
        for other in range(2):
            value = jnp.concatenate([parts[2 * other], parts[2 * other + 1]], axis=1)
            if step:
                value = pltpu.roll(value, 256 - step, 1)
            matrix = spread_ref[other * 256 : (other + 1) * 256, :].astype(BF16)
            for _ in range(3):
                part = value.astype(BF16)
                value = value - part.astype(F32)
                term = mm(part, matrix)
                total = term if total is None else total + term
        for half in range(2):
            stage[half, pl.ds(step, TOK, stride=12), :] = total[:, half * 128 : half * 128 + 128]
    for lev in range(2):
        closed = masks_ref[1] * last
        if lev == 1:
            closed = closed + masks_ref[0]
        for h in range(HEADS):
            rows = slice((2 * h + lev) * TOK, (2 * h + lev + 1) * TOK)
            value = jnp.concatenate([stage[0, rows, :], stage[1, rows, 0:16]], axis=1)
            bias[lev, h * TOK : (h + 1) * TOK, :] = jnp.where(closed > 0.5, -1000000000.0, value)


def reduce_table(d_bias, spread_ref, parts, flat, table):
    sums = [None, None]
    for step in range(12):
        value = jnp.concatenate(
            [d_bias[half, pl.ds(step, TOK, stride=12), :] for half in range(2)], axis=1
        )
        high = value.astype(BF16)
        low = (value - high.astype(F32)).astype(BF16)
        for other in range(2):
            matrix = spread_ref[other * 256 : (other + 1) * 256, :].astype(BF16)
            term = mm_nt(high, matrix) + mm_nt(low, matrix)
            if step:
                sums[other] = sums[other] + pltpu.roll(term, step, 1)
            else:
                sums[other] = term
    for other in range(2):
        for half in range(2):
            parts[2 * other + half] = sums[other][:, half * 128 : half * 128 + 128]
    flat[...] = jnp.zeros_like(flat)
    for cell in range(12):
        for other in range(2):
            start = segment(cell, other)
            rows = pl.ds(cell, 12, stride=12)
            flat[0:12, start : start + 128] = parts[2 * other, rows, :]
            flat[0:12, start + 128 : start + SEG] = parts[2 * other + 1, rows, :][:, 0 : SEG - 128]
    for part in range(16):
        table[part * 16 : (part + 1) * 16, :] = flat[:, part * 256 : (part + 1) * 256]


def gather_all(own, below, edges, place, place_edge, out):
    place = place[...].astype(BF16)
    for lev in range(4):
        source = (lev + 1) % 4
        parts = [
            own[source, 3:6].astype(F32).reshape(72, C),
            below[source].astype(F32).reshape(72, C),
        ]
        rows = mm(place, jnp.concatenate(parts, axis=0).astype(BF16))
        rows = rows + mm(place_edge[lev].astype(BF16), edges[...])
        for half in range(2):
            start = ((lev // 2) * 2 + half) * TOK + (lev % 2) * 72
            out[start : start + 72, :] = rows[half * 72 : (half + 1) * 72, :].astype(out.dtype)


def scatter_all(value, place, pick, own, full, edges):
    place = place[...].astype(BF16)
    for lev in range(4):
        parts = []
        for half in range(2):
            start = ((lev // 2) * 2 + half) * TOK + (lev % 2) * 72
            parts.append(value[start : start + 72, :])
        rows = mm(place, jnp.concatenate(parts, axis=0).astype(BF16))
        own[lev] = rows[0:72].reshape(3, 24, C).astype(BF16)
        full[lev] = rows[72:144].reshape(3, 24, C).astype(BF16)
    edges[...] = mm(pick[...].astype(BF16), value[...].astype(BF16)).astype(BF16)


INPUTS = (
    "fields",
    "cotangent",
    "bias_table",
    "gain_one",
    "w_qkv",
    "w_proj",
    "gain_two",
    "w_in",
    "w_out",
    "place_in",
    "edge_in",
    "pick_in",
    "place_out",
    "pick_out",
    "spread",
    "masks",
    "heads",
)


class Section:
    def __init__(self, net, chunk, rest, refs):
        self.net, self.chunk, self.rest = net, chunk, rest
        (
            self.pack,
            self.table,
            self.send_pair,
            self.recv_pair,
            self.send_lon,
            self.recv_lon,
            self.total,
            self.by_lat,
            self.gathered,
            self.sems,
        ) = refs
        self.pair, self.along_lon, self.along_lat = [], [], []

    def rows(self, ref, size, core, k):
        start = pl.multiple_of((2 * k + core) * size, size)
        return ref[pl.ds(start, size), :]

    def sem(self, stage, slot):
        return (self.sems.at[stage, slot], self.sems.at[stage + 1, slot])

    def to_pair(self):
        net = self.net
        for d in range(1, net.n_k + 1):
            k = lax.rem(net.k + d, net.n_k)
            self.send_pair[d - 1, 0 : self.chunk, :] = self.rows(
                self.pack, self.chunk, net.other, k
            ).astype(BF16)
            if self.rest:
                self.send_pair[d - 1, self.chunk : self.chunk + self.rest, :] = self.rows(
                    self.table, self.rest, net.other, k
                ).astype(BF16)
            self.pair.append(
                net.start(
                    self.send_pair.at[d - 1],
                    self.recv_pair.at[d - 1],
                    self.sem(0, d - 1),
                    net.partner,
                )
            )

    def to_lon(self):
        net = self.net
        for d in range(1, net.n_k + 1):
            k = lax.rem(net.k + d, net.n_k)
            self.pair[d - 1].wait_recv()
            value = self.rows(self.pack, self.chunk, net.core, k)
            if self.rest:
                value = jnp.concatenate(
                    [value, self.rows(self.table, self.rest, net.core, k)], axis=0
                )
            value = value + self.recv_pair[d - 1].astype(F32)
            if d == net.n_k:
                self.total[...] = value
                continue
            self.send_lon[d - 1] = value.astype(BF16)
            self.along_lon.append(
                net.start(
                    self.send_lon.at[d - 1],
                    self.recv_lon.at[d - 1],
                    self.sem(2, d - 1),
                    net.along_lon(d),
                )
            )

    def to_lat(self):
        net = self.net
        value = self.total[...]
        for d in range(1, net.n_k):
            self.along_lon[d - 1].wait_recv()
            value = value + self.recv_lon[d - 1].astype(F32)
        value = value.astype(BF16)
        mine = self.by_lat.at[net.lat]
        mine[...] = value[0 : self.chunk, :]
        if self.rest:
            self.gathered[net.core, net.k, self.chunk : self.chunk + self.rest, :] = value[
                self.chunk : self.chunk + self.rest, :
            ]
        for d in range(1, net.n_l):
            self.along_lat.append(net.start(mine, mine, self.sem(4, d - 1), net.along_lat(d)))

    def spread_lon(self):
        net = self.net
        for d in range(1, net.n_l):
            theirs = self.by_lat.at[lax.rem(net.lat - d + net.n_l, net.n_l)]
            net.copy(theirs, theirs, self.sem(4, d - 1), net.partner).wait_recv()
        value = self.by_lat[0].astype(F32)
        for i in range(1, net.n_l):
            value = value + self.by_lat[i].astype(F32)
        self.gathered[net.core, net.k, 0 : self.chunk, :] = value.astype(BF16)
        mine = self.gathered.at[net.core, net.k]
        for d in range(1, net.n_k):
            net.start(mine, mine, self.sem(6, d - 1), net.along_lon(d))
        net.start(mine, mine, self.sem(8, 0), net.partner)

    def spread_pair(self):
        net = self.net
        for d in range(1, net.n_k):
            theirs = self.gathered.at[net.core, lax.rem(net.k - d + net.n_k, net.n_k)]
            net.copy(theirs, theirs, self.sem(6, d - 1), net.partner).wait_recv()
            net.start(theirs, theirs, self.sem(8, d), net.partner)

    def close(self):
        net = self.net
        for d in range(net.n_k):
            theirs = self.gathered.at[net.other, lax.rem(net.k - d + net.n_k, net.n_k)]
            net.copy(theirs, theirs, self.sem(8, d), net.partner).wait_recv()


class Net:
    def __init__(self, n_k, n_l):
        self.n_k, self.n_l = n_k, n_l
        self.n_lon = 2 * n_k
        self.lon, self.lat = lax.axis_index("lon"), lax.axis_index("lat")
        self.core, self.k = lax.rem(self.lon, 2), self.lon // 2
        self.other = 1 - self.core
        self.partner = (2 * self.k + self.other, self.lat)
        self.started = []

    def at(self, d_lon, d_lat):
        return (
            lax.rem(self.lon + d_lon + self.n_lon, self.n_lon),
            lax.rem(self.lat + d_lat + self.n_l, self.n_l),
        )

    def along_lon(self, d):
        return (2 * lax.rem(self.k + d, self.n_k) + self.core, self.lat)

    def along_lat(self, d):
        return self.at(0, d)

    def greet(self):
        far = lax.rem(self.lon + 2 * self.core - 1 + self.n_lon, self.n_lon)
        friends = [self.partner, (far, self.lat), self.at(1, 1), self.at(-1, -1)]
        friends += [self.along_lon(d) for d in range(1, self.n_k)]
        friends += [self.along_lat(d) for d in range(1, self.n_l)]
        barrier = pltpu.get_barrier_semaphore()
        for friend in friends:
            pl.semaphore_signal(barrier, inc=1, device_id=friend, device_id_type=MESH)
        return barrier, len(friends)

    def copy(self, source, target, sems, device):
        return pltpu.make_async_remote_copy(
            src_ref=source,
            dst_ref=target,
            send_sem=sems[0],
            recv_sem=sems[1],
            device_id=device,
            device_id_type=MESH,
        )

    def start(self, source, target, sems, device):
        c = self.copy(source, target, sems, device)
        c.start()
        self.started.append(c)
        return c


def block_kernel(n_k, n_l, *refs):
    refs = list(refs)

    def take(count):
        out = refs[:count]
        del refs[:count]
        return out

    hbm = dict(zip(INPUTS, take(len(INPUTS)), strict=True))
    early_out, late_out, own_out, below_out, edge_out = take(5)
    here = dict(zip(INPUTS, take(len(INPUTS)), strict=True))
    below, edges, edges_send, full, edges_back = take(5)
    x_ref, cot_ref, n1_ref, q_ref, k_ref, v_ref, bias, probs, att_ref = take(9)
    act_ref, dpre_ref, n2_ref, dbb_ref, dbranch_ref, datt_ref, out_ref = take(7)
    dq_ref, dk_ref, dv_ref, d_bias, parts, stage, flat = take(7)
    early_pack, late_pack, table = take(3)
    early_bufs, late_bufs = take(6), take(6)
    load_sem, in_sem, out_sem, early_sem, late_sem = take(5)

    net = Net(n_k, n_l)
    barrier, count = net.greet()
    loads = {
        name: pltpu.make_async_copy(hbm[name], here[name], load_sem.at[i])
        for i, name in enumerate(INPUTS)
    }
    for name in INPUTS:
        loads[name].start()

    early = Section(net, EARLY // net.n_lon, 0, [early_pack, None, *early_bufs, early_out, early_sem])
    late = Section(
        net,
        LATE // net.n_lon,
        TABLE // net.n_lon,
        [late_pack, table, *late_bufs, late_out, late_sem],
    )

    def send_in(i, name):
        south = net.start(
            hbm[name].at[:, 0:3], below.at[i], (in_sem.at[0, i, 0], in_sem.at[1, i, 0]), net.at(0, -1)
        )
        flat_rows = here[name][...].astype(F32).reshape(ROWS, C).astype(BF16)
        edges_send[i] = mm(here["pick_in"][...].astype(BF16), flat_rows).astype(BF16)
        east = net.start(
            edges_send.at[i, 0:EDGE],
            edges.at[i, 0:EDGE],
            (in_sem.at[0, i, 1], in_sem.at[1, i, 1]),
            net.at(-1, 0),
        )
        corner = net.start(
            edges_send.at[i, EDGE : 2 * EDGE],
            edges.at[i, EDGE : 2 * EDGE],
            (in_sem.at[0, i, 2], in_sem.at[1, i, 2]),
            net.at(-1, -1),
        )
        return [south, east, corner]

    def send_out(i):
        return [
            net.start(
                full.at[i], below_out.at[i], (out_sem.at[0, i, 0], out_sem.at[1, i, 0]), net.at(0, 1)
            ),
            net.start(
                edges_back.at[i, 0:EDGE],
                edge_out.at[i, 0:EDGE],
                (out_sem.at[0, i, 1], out_sem.at[1, i, 1]),
                net.at(1, 0),
            ),
            net.start(
                edges_back.at[i, EDGE : 2 * EDGE],
                edge_out.at[i, EDGE : 2 * EDGE],
                (out_sem.at[0, i, 2], out_sem.at[1, i, 2]),
                net.at(1, 1),
            ),
        ]

    for name in INPUTS:
        loads[name].wait()
    pl.semaphore_wait(barrier, count)
    in_copies = [send_in(0, "fields")]

    last = (net.lat == n_l - 1).astype(F32)
    expand_bias(here["bias_table"], here["spread"], here["masks"], parts, flat, stage, bias, last)

    heads32 = here["heads"][...]
    heads = heads32.astype(BF16)
    scale = 32**-0.5
    gain1 = here["gain_one"][...]
    gain2 = here["gain_two"][...]
    w_qkv, w_proj, w_in, w_out = here["w_qkv"], here["w_proj"], here["w_in"], here["w_out"]

    for c in in_copies[0]:
        c.wait_recv()
    in_copies.append(send_in(1, "cotangent"))
    gather_all(here["fields"], below.at[0], edges.at[0], here["place_in"], here["edge_in"], x_ref)
    unit, _ = norm(x_ref[...])
    n1 = (unit * gain1).astype(BF16)
    n1_ref[...] = n1
    for i, ref in enumerate((q_ref, k_ref, v_ref)):
        ref[...] = mm(n1, w_qkv[:, i * C : (i + 1) * C]).astype(BF16)

    def attend(w, carry):
        rows = pl.ds(pl.multiple_of(w * TOK, TOK), TOK)
        stacked = split_heads(q_ref[rows, :], heads)
        scores = mm_nt(stacked, k_ref[rows, :]) * scale + bias[w // 2]
        top = jnp.max(scores, axis=-1, keepdims=True)
        exps = jnp.exp(scores - top)
        prob = exps * (1.0 / jnp.sum(exps, axis=-1, keepdims=True))
        probs[w] = prob
        mixed = mm(prob.astype(BF16), v_ref[rows, :])
        att_ref[rows, :] = join_heads(mixed, heads32).astype(BF16)
        return carry

    lax.fori_loop(0, WIN, attend, 0)

    for c in in_copies[1]:
        c.wait_recv()
    gather_all(
        here["cotangent"], below.at[1], edges.at[1], here["place_in"], here["edge_in"], cot_ref
    )
    half = ROWS // 2

    def feed(i, gain_sum):
        rows = pl.ds(pl.multiple_of(i * half, half), half)
        branch = x_ref[rows, :] + mm(att_ref[rows, :], w_proj[...])
        unit, inverse = norm(branch)
        n2 = (unit * gain2).astype(BF16)
        n2_ref[rows, :] = n2
        pre = mm(n2, w_in[...])
        cdf = 0.5 + 0.5 * lax.erf(pre * (0.5**0.5))
        slope = cdf + pre * (jnp.exp(-0.5 * pre * pre) * ((2.0 * np.pi) ** -0.5))
        act = (pre * cdf).astype(BF16)
        act_ref[rows, :] = act
        out_ref[rows, :] = branch + mm_nt(act, w_out[...])
        cot = cot_ref[rows, :]
        d_pre = (slope * mm(cot, w_out[...])).astype(BF16)
        dpre_ref[rows, :] = d_pre
        d_normed = mm_nt(d_pre, w_in[...])
        d_branch = cot.astype(F32) + norm_grad(d_normed, gain2, unit, inverse)
        dbranch_ref[rows, :] = d_branch
        dbb = d_branch.astype(BF16)
        dbb_ref[rows, :] = dbb
        datt_ref[rows, :] = mm_nt(dbb, w_proj[...]).astype(BF16)
        return gain_sum + jnp.sum(d_normed * unit, axis=0, keepdims=True)

    gain_sum2 = lax.fori_loop(0, 2, feed, jnp.zeros((1, C), F32))

    early_pack[1152:EARLY, 128:256] = jnp.zeros((EARLY - 1152, 128), F32)
    early_pack[1344:EARLY, 0:128] = jnp.zeros((EARLY - 1344, 128), F32)
    early_pack[1344:1345, 0:C] = gain_sum2
    for i in range(3):
        cols = slice(i * 256, (i + 1) * 256)
        early_pack[i * C : (i + 1) * C, :] = mm_tn(cot_ref[...], act_ref[:, cols])
        early_pack[576 + i * C : 576 + (i + 1) * C, :] = mm_tn(n2_ref[...], dpre_ref[:, cols])
    early_pack[1152 : 1152 + C, 0:C] = mm_tn(att_ref[...], dbb_ref[...])
    early.to_pair()
    scatter_all(
        out_ref, here["place_out"], here["pick_out"], own_out.at[0], full.at[0], edges_back.at[0]
    )
    out_copies = send_out(0)

    d_bias[...] = jnp.zeros_like(d_bias)

    def attend_back(w, carry):
        rows = pl.ds(pl.multiple_of(w * TOK, TOK), TOK)
        prob = probs[w]
        d_stacked = split_heads(datt_ref[rows, :], heads)
        d_prob = mm_nt(d_stacked, v_ref[rows, :])
        d_score = prob * (d_prob - jnp.sum(d_prob * prob, axis=-1, keepdims=True))
        for h in range(HEADS):
            group = pl.ds(pl.multiple_of((2 * h + w // 2) * TOK, TOK), TOK)
            part = d_score[h * TOK : (h + 1) * TOK, :]
            d_bias[0, group, :] += part[:, 0:128]
            d_bias[1, group, 0:16] += part[:, 128:144]
        d_score_b = d_score.astype(BF16)
        dv_ref[rows, :] = mm_tn(prob.astype(BF16), d_stacked).astype(BF16)
        dq_ref[rows, :] = (join_heads(mm(d_score_b, k_ref[rows, :]), heads32) * scale).astype(BF16)
        stacked = split_heads(q_ref[rows, :], heads)
        dk_ref[rows, :] = (mm_tn(d_score_b, stacked) * scale).astype(BF16)
        return carry

    lax.fori_loop(0, WIN // 2, attend_back, 0)
    early.to_lon()
    lax.fori_loop(WIN // 2, WIN, attend_back, 0)

    d_normed = None
    late_pack[:, 128:256] = jnp.zeros((LATE, 128), F32)
    late_pack[576:LATE, 0:128] = jnp.zeros((LATE - 576, 128), F32)
    for i, ref in enumerate((dq_ref, dk_ref, dv_ref)):
        late_pack[i * C : (i + 1) * C, 0:C] = mm_tn(n1_ref[...], ref[...])
        term = mm_nt(ref[...], w_qkv[:, i * C : (i + 1) * C])
        d_normed = term if d_normed is None else d_normed + term
    unit, inverse = norm(x_ref[...])
    late_pack[576:577, 0:C] = jnp.sum(d_normed * unit, axis=0, keepdims=True)
    out_ref[...] = dbranch_ref[...] + norm_grad(d_normed, gain1, unit, inverse)
    reduce_table(d_bias, here["spread"], parts, flat, table)
    late.to_pair()
    early.to_lat()
    late.to_lon()
    scatter_all(
        out_ref, here["place_out"], here["pick_out"], own_out.at[1], full.at[1], edges_back.at[1]
    )
    out_copies += send_out(1)
    early.spread_lon()
    late.to_lat()
    late.spread_lon()
    early.spread_pair()
    late.spread_pair()
    early.close()
    late.close()
    for c in out_copies:
        c.wait_recv()
    for c in net.started:
        c.wait_send()


def finish_kernel(
    n_k,
    early,
    late,
    own_out,
    below_out,
    edge_out,
    place_end,
    edge_end,
    block_out,
    grad_fields,
    g_gain_one,
    g_w_qkv,
    g_table,
    g_w_proj,
    g_gain_two,
    g_w_in,
    g_w_out,
    early_rows,
    late_rows,
):
    n_lon = 2 * n_k
    place = place_end[...].astype(BF16)
    for i, ref in enumerate((block_out, grad_fields)):
        for lev in range(4):
            parts = [
                below_out[i, lev].astype(F32).reshape(72, C),
                own_out[i, lev].astype(F32).reshape(72, C),
            ]
            rows = mm(place, jnp.concatenate(parts, axis=0).astype(BF16))
            rows = rows + mm(edge_end[lev].astype(BF16), edge_out[i])
            ref[(lev + 1) % 4] = rows.reshape(6, 24, C).astype(BF16)
    for source, target, size in ((early, early_rows, EARLY), (late, late_rows, LATE)):
        chunk = size // n_lon
        for part in range(n_lon):
            target[part * chunk : (part + 1) * chunk, :] = source[
                part % 2, part // 2, 0:chunk, :
            ].astype(F32)
    for i in range(3):
        cols = slice(i * 256, (i + 1) * 256)
        g_w_out[:, cols] = early_rows[i * C : (i + 1) * C, :]
        g_w_in[:, cols] = early_rows[576 + i * C : 576 + (i + 1) * C, :]
        g_w_qkv[:, i * C : (i + 1) * C] = late_rows[i * C : (i + 1) * C, 0:C]
    g_w_proj[...] = early_rows[1152 : 1152 + C, 0:C]
    g_gain_two[...] = early_rows[1344:1345, 0:C]
    g_gain_one[...] = late_rows[576:577, 0:C]
    rest, chunk = TABLE // n_lon, LATE // n_lon
    for part in range(13):
        width = min(256, POS - part * 256)
        place, offset = divmod(part * 16, rest)
        value = late[place % 2, place // 2, chunk + offset : chunk + offset + 16, :].astype(F32)
        for h in range(HEADS):
            g_table[0, h, :, part * 256 : part * 256 + width] = value[2 * h : 2 * h + 2, 0:width]


def local(n_k, n_l, fields, cotangent, bias_table, gain_one, w_qkv, w_proj, gain_two, w_in, w_out):
    n_lon = 2 * n_k
    sds = jax.ShapeDtypeStruct
    vmem = pltpu.VMEM
    dma = pltpu.SemaphoreType.DMA
    whole = pl.BlockSpec(memory_space=pltpu.VMEM)
    apart = pl.BlockSpec(memory_space=pl.ANY)
    early, late = EARLY // n_lon, LATE // n_lon
    both = late + TABLE // n_lon
    inputs = (
        fields,
        cotangent,
        bias_table.transpose(0, 2, 1, 3),
        gain_one.reshape(1, C),
        w_qkv,
        w_proj,
        gain_two.reshape(1, C),
        w_in,
        w_out.T,
        jnp.asarray(place_level_in()),
        jnp.asarray(place_edge_in()),
        jnp.asarray(pick_edge_in()),
        jnp.asarray(place_level_out()),
        jnp.asarray(pick_edge_out()),
        jnp.asarray(spread_matrix()),
        jnp.asarray(region_masks()),
        jnp.asarray(head_masks()),
    )

    def buffers(chunk, kept):
        return [
            vmem((n_k, chunk, 256), BF16),
            vmem((n_k, chunk, 256), BF16),
            vmem((n_k - 1, chunk, 256), BF16),
            vmem((n_k - 1, chunk, 256), BF16),
            vmem((chunk, 256), F32),
            vmem((n_l, kept, 256), BF16),
        ]

    slots = max(n_k, n_l)
    results = pl.pallas_call(
        functools.partial(block_kernel, n_k, n_l),
        out_shape=(
            sds((2, n_k, early, 256), BF16),
            sds((2, n_k, both, 256), BF16),
            sds((2, 4, 3, 24, C), BF16),
            sds((2, 4, 3, 24, C), BF16),
            sds((2, 2 * EDGE, C), BF16),
        ),
        in_specs=[apart] * len(INPUTS),
        out_specs=[whole] * 5,
        scratch_shapes=[vmem(value.shape, value.dtype) for value in inputs]
        + [
            vmem((2, 4, 3, 24, C), BF16),
            vmem((2, 2 * EDGE, C), BF16),
            vmem((2, 2 * EDGE, C), BF16),
            vmem((2, 4, 3, 24, C), BF16),
            vmem((2, 2 * EDGE, C), BF16),
            vmem((ROWS, C), F32),
            vmem((ROWS, C), BF16),
            vmem((ROWS, C), BF16),
            vmem((ROWS, C), BF16),
            vmem((ROWS, C), BF16),
            vmem((ROWS, C), BF16),
            vmem((2, STACK, TOK), F32),
            vmem((WIN, STACK, TOK), F32),
            vmem((ROWS, C), BF16),
            vmem((ROWS, FFH), BF16),
            vmem((ROWS, FFH), BF16),
            vmem((ROWS, C), BF16),
            vmem((ROWS, C), BF16),
            vmem((ROWS, C), F32),
            vmem((ROWS, C), BF16),
            vmem((ROWS, C), F32),
            vmem((ROWS, C), BF16),
            vmem((ROWS, C), BF16),
            vmem((ROWS, C), BF16),
            vmem((2, 2 * STACK, 128), F32),
            vmem((4, TOK, 128), F32),
            vmem((2, 2 * STACK, 128), F32),
            vmem((16, 4096), F32),
            vmem((EARLY, 256), F32),
            vmem((LATE, 256), F32),
            vmem((TABLE, 256), F32),
        ]
        + buffers(early, early)
        + buffers(both, late)
        + [
            dma((len(INPUTS),)),
            dma((2, 2, 3)),
            dma((2, 2, 3)),
            dma((10, slots)),
            dma((10, slots)),
        ],
        compiler_params=pltpu.CompilerParams(
            collective_id=0, has_side_effects=True, vmem_limit_bytes=60 * 1024 * 1024
        ),
        name="block",
    )(*inputs)
    outs = pl.pallas_call(
        functools.partial(finish_kernel, n_k),
        out_shape=(
            sds((4, 6, 24, C), BF16),
            sds((4, 6, 24, C), BF16),
            sds((1, C), F32),
            sds((C, 3 * C), F32),
            sds((1, HEADS, 2, POS), F32),
            sds((C, C), F32),
            sds((1, C), F32),
            sds((C, FFH), F32),
            sds((C, FFH), F32),
        ),
        in_specs=[whole] * 7,
        out_specs=[whole] * 9,
        scratch_shapes=[vmem((EARLY, 256), F32), vmem((LATE, 256), F32)],
        compiler_params=pltpu.CompilerParams(vmem_limit_bytes=60 * 1024 * 1024),
        name="finish",
    )(*results, jnp.asarray(place_level_end()), jnp.asarray(place_edge_end()))
    outs = list(outs)
    outs[2] = outs[2].reshape(C)
    outs[4] = outs[4].transpose(0, 2, 1, 3)
    outs[6] = outs[6].reshape(C)
    outs[8] = outs[8].T
    return tuple(outs)


def solution(mesh):
    n_k, n_l = mesh.shape["lon"] // 2, mesh.shape["lat"]
    placed = (
        P(None, "lat", "lon", None),
        P(None, "lat", "lon", None),
        P("lat", None, None, None),
    ) + (P(),) * 6
    return jax.shard_map(
        functools.partial(local, n_k, n_l),
        mesh=mesh,
        in_specs=placed,
        out_specs=(
            P(None, "lat", "lon", None),
            P(None, "lat", "lon", None),
            P(),
            P(),
            P("lat", None, None, None),
            P(),
            P(),
            P(),
            P(),
        ),
        check_vma=False,
    )
```

time: 80.4 us -> 70 us (0.87)
  local copies, waits for them, and re-layouts: 10.5 us -> 0 us
    unnamed x16 -> x0, local copies, waits for them, and re-layouts: 10.5 us -> none
    pallas_call x1, Pallas kernels: 1.49 us -> 3.54 us  [local(): pl.pallas_call(functools.partial(finish_kernel, n_k), out_shape=(sds((4,...]
    pallas_call x1, Pallas kernels: 67.4 us -> 65.7 us  [local(): pl.pallas_call(functools.partial(block_kernel, n_k, n_l), out_shape=(sds(...]
where the time goes in v2:
time: 70 us; the launch traced here: 69.9 us
  Pallas kernels  69.2 us (99%)
    pallas_call x1, Pallas kernels, local(): pl.pallas_call(functools.partial(block_kernel, n_k, n_l), out_shape=(sds(...  65.7 us
    pallas_call x1, Pallas kernels, local(): pl.pallas_call(functools.partial(finish_kernel, n_k), out_shape=(sds((4,...  3.54 us

profile of v2, /device:TPU:1, one launch (start us, length us, event | category | flops | bytes accessed | tf_op | source)
XLA Modules:
  0.0 69.9 jit_solution(17161595767660395398)
XLA Ops:
  0.6 65.7 %block.1 = (bf16[2,8,96,256]{3,2,1,0:T(8,128)(2,1)}, bf16[2,8,64,256]{3,2,1,0:T(8,128)(2,1)}, bf16[2,4,3,24,192]{4,3,2,1,0:T(8,128)(2,1)}, bf16[2,4,3,24,192]{4,3,2,1,0:T(8,128)(2,1)}, bf16[2,160,192]{2,1,0:T(8,128)(2,1)}) custom-call(bf16[4,6,24,192]{3,2,1,0:T(8,128)(2,1)} %refs_0_.1, bf16[4,6,24,192]{3,2,1,0:T(8,128)(2,1)} %refs_1_.1, ...), custom_call_target="tpu_custom_call" | custom-call | tf_op jit(solution)/shard_map/block/pallas_call | solution.py:751
  66.3 3.5 %finish.1 = (bf16[4,6,24,192]{3,2,1,0:T(8,128)(2,1)}, bf16[4,6,24,192]{3,2,1,0:T(8,128)(2,1)}, f32[1,192]{1,0:T(1,128)}, f32[192,576]{1,0:T(8,128)}, f32[1,6,2,3...) custom-call(bf16[2,8,96,256]{3,2,1,0:T(8,128)(2,1)} %get-tuple-element.2, ...), custom_call_target="tpu_custom_call" | custom-call | tf_op jit(solution)/shard_map/finish/pallas_call | solution.py:810

commit v3 on v2

--- a/solution.py
+++ b/solution.py
@@ -18,7 +18,7 @@
 POS = 3312
 SEG = 138
 EARLY = 1536
-LATE = 768
+LATE = 512
 TABLE = 256
 EDGE = 80
 MESH = pl.DeviceIdType.MESH
@@ -200,20 +200,22 @@
 
 
 def reduce_table(d_bias, spread_ref, parts, flat, table):
-    sums = [None, None]
-    for step in range(12):
-        value = jnp.concatenate(
-            [d_bias[half, pl.ds(step, TOK, stride=12), :] for half in range(2)], axis=1
-        )
-        high = value.astype(BF16)
-        low = (value - high.astype(F32)).astype(BF16)
-        for other in range(2):
-            matrix = spread_ref[other * 256 : (other + 1) * 256, :].astype(BF16)
-            term = mm_nt(high, matrix) + mm_nt(low, matrix)
-            if step:
-                sums[other] = sums[other] + pltpu.roll(term, step, 1)
-            else:
-                sums[other] = term
+    value = jnp.concatenate(
+        [
+            jnp.concatenate(
+                [d_bias[half, pl.ds(step, TOK, stride=12), :] for half in range(2)], axis=1
+            )
+            for step in range(12)
+        ],
+        axis=0,
+    ).astype(BF16)
+    sums = []
+    for other in range(2):
+        terms = mm_nt(value, spread_ref[other * 256 : (other + 1) * 256, :].astype(BF16))
+        total = terms[0:TOK, :]
+        for step in range(1, 12):
+            total = total + pltpu.roll(terms[step * TOK : (step + 1) * TOK, :], step, 1)
+        sums.append(total)
     for other in range(2):
         for half in range(2):
             parts[2 * other + half] = sums[other][:, half * 128 : half * 128 + 128]
@@ -289,10 +291,11 @@
             self.recv_lon,
             self.total,
             self.by_lat,
+            self.send_lat,
             self.gathered,
             self.sems,
         ) = refs
-        self.pair, self.along_lon, self.along_lat = [], [], []
+        self.pair, self.along_lon = [], []
 
     def rows(self, ref, size, core, k):
         start = pl.multiple_of((2 * k + core) * size, size)
@@ -345,48 +348,122 @@
                 )
             )
 
-    def to_lat(self):
-        net = self.net
+    def sum_lon(self):
         value = self.total[...]
-        for d in range(1, net.n_k):
+        for d in range(1, self.net.n_k):
             self.along_lon[d - 1].wait_recv()
             value = value + self.recv_lon[d - 1].astype(F32)
-        value = value.astype(BF16)
+        return value.astype(BF16)
+
+    def sum_lat(self):
+        value = self.by_lat[0].astype(F32)
+        for i in range(1, self.net.n_l):
+            value = value + self.by_lat[i].astype(F32)
+        return value.astype(BF16)
+
+    def spread_lon(self):
+        net = self.net
+        mine = self.gathered.at[net.core, net.k]
+        for d in range(1, net.n_k):
+            net.start(mine, mine, self.sem(8, d - 1), net.along_lon(d))
+        net.start(mine, mine, self.sem(10, 0), net.partner)
+
+    def to_lat(self):
+        net = self.net
+        value = self.sum_lon()
         mine = self.by_lat.at[net.lat]
         mine[...] = value[0 : self.chunk, :]
-        if self.rest:
-            self.gathered[net.core, net.k, self.chunk : self.chunk + self.rest, :] = value[
-                self.chunk : self.chunk + self.rest, :
-            ]
+        self.gathered[net.core, net.k, self.chunk : self.chunk + self.rest, :] = value[
+            self.chunk : self.chunk + self.rest, :
+        ]
         for d in range(1, net.n_l):
-            self.along_lat.append(net.start(mine, mine, self.sem(4, d - 1), net.along_lat(d)))
-
-    def spread_lon(self):
+            net.start(mine, mine, self.sem(4, d - 1), net.along_lat(d))
+
+    def from_lat(self):
         net = self.net
         for d in range(1, net.n_l):
             theirs = self.by_lat.at[lax.rem(net.lat - d + net.n_l, net.n_l)]
             net.copy(theirs, theirs, self.sem(4, d - 1), net.partner).wait_recv()
-        value = self.by_lat[0].astype(F32)
-        for i in range(1, net.n_l):
-            value = value + self.by_lat[i].astype(F32)
-        self.gathered[net.core, net.k, 0 : self.chunk, :] = value.astype(BF16)
-        mine = self.gathered.at[net.core, net.k]
-        for d in range(1, net.n_k):
-            net.start(mine, mine, self.sem(6, d - 1), net.along_lon(d))
-        net.start(mine, mine, self.sem(8, 0), net.partner)
+        self.gathered[net.core, net.k, 0 : self.chunk, :] = self.sum_lat()
+        self.spread_lon()
+
+    def to_owner(self, pieces):
+        net = self.net
+        value = self.sum_lon()
+        for p in range(pieces):
+            pieces_ref = self.send_lat.at[p]
+            pieces_ref[...] = value[p * 16 : (p + 1) * 16, :]
+
+            @pl.when(net.lat != p)
+            def _(p=p):
+                self.owner_copy(p).start()
+
+    def owner_copy(self, p):
+        net = self.net
+        sems = (self.sems.at[4, p], self.sems.at[5, net.lat])
+        return net.copy(self.send_lat.at[p], self.by_lat.at[net.lat], sems, (net.lon, p))
+
+    def own_piece(self):
+        net = self.net
+        return self.gathered.at[net.core, net.k, pl.ds(pl.multiple_of(net.lat * 16, 16), 16), :]
+
+    def back_copy(self, d):
+        net = self.net
+        sems = (self.sems.at[6, d - 1], self.sems.at[7, net.lat])
+        return net.copy(self.own_piece(), self.own_piece(), sems, net.along_lat(d))
+
+    def from_owner(self, pieces):
+        net = self.net
+
+        @pl.when(net.lat < pieces)
+        def _():
+            self.by_lat[net.lat] = self.send_lat[net.lat]
+            for d in range(1, net.n_l):
+                source = lax.rem(net.lat + d, net.n_l)
+                theirs = self.by_lat.at[source]
+                sems = (self.sems.at[4, 0], self.sems.at[5, source])
+                net.copy(theirs, theirs, sems, net.partner).wait_recv()
+            self.own_piece()[...] = self.sum_lat()
+            for d in range(1, net.n_l):
+                self.back_copy(d).start()
+
+    def after_owner(self, pieces):
+        net = self.net
+        for p in range(pieces):
+
+            @pl.when(net.lat != p)
+            def _(p=p):
+                theirs = self.gathered.at[net.core, net.k, p * 16 : (p + 1) * 16, :]
+                sems = (self.sems.at[6, 0], self.sems.at[7, p])
+                net.copy(theirs, theirs, sems, net.partner).wait_recv()
+
+        self.spread_lon()
+
+    def close_owner(self, pieces):
+        net = self.net
+        for p in range(pieces):
+
+            @pl.when(net.lat != p)
+            def _(p=p):
+                self.owner_copy(p).wait_send()
+
+        @pl.when(net.lat < pieces)
+        def _():
+            for d in range(1, net.n_l):
+                self.back_copy(d).wait_send()
 
     def spread_pair(self):
         net = self.net
         for d in range(1, net.n_k):
             theirs = self.gathered.at[net.core, lax.rem(net.k - d + net.n_k, net.n_k)]
-            net.copy(theirs, theirs, self.sem(6, d - 1), net.partner).wait_recv()
-            net.start(theirs, theirs, self.sem(8, d), net.partner)
+            net.copy(theirs, theirs, self.sem(8, d - 1), net.partner).wait_recv()
+            net.start(theirs, theirs, self.sem(10, d), net.partner)
 
     def close(self):
         net = self.net
         for d in range(net.n_k):
             theirs = self.gathered.at[net.other, lax.rem(net.k - d + net.n_k, net.n_k)]
-            net.copy(theirs, theirs, self.sem(8, d), net.partner).wait_recv()
+            net.copy(theirs, theirs, self.sem(10, d), net.partner).wait_recv()
 
 
 class Net:
@@ -454,7 +531,7 @@
     act_ref, dpre_ref, n2_ref, dbb_ref, dbranch_ref, datt_ref, out_ref = take(7)
     dq_ref, dk_ref, dv_ref, d_bias, parts, stage, flat = take(7)
     early_pack, late_pack, table = take(3)
-    early_bufs, late_bufs = take(6), take(6)
+    early_bufs, late_bufs = take(7), take(7)
     load_sem, in_sem, out_sem, early_sem, late_sem = take(5)
 
     net = Net(n_k, n_l)
@@ -478,6 +555,9 @@
         south = net.start(
             hbm[name].at[:, 0:3], below.at[i], (in_sem.at[0, i, 0], in_sem.at[1, i, 0]), net.at(0, -1)
         )
+        if i == 0:
+            loads["fields"].wait()
+            loads["pick_in"].wait()
         flat_rows = here[name][...].astype(F32).reshape(ROWS, C).astype(BF16)
         edges_send[i] = mm(here["pick_in"][...].astype(BF16), flat_rows).astype(BF16)
         east = net.start(
@@ -513,10 +593,11 @@
             ),
         ]
 
-    for name in INPUTS:
-        loads[name].wait()
     pl.semaphore_wait(barrier, count)
     in_copies = [send_in(0, "fields")]
+    for name in INPUTS:
+        if name not in ("fields", "pick_in"):
+            loads[name].wait()
 
     last = (net.lat == n_l - 1).astype(F32)
     expand_bias(here["bias_table"], here["spread"], here["masks"], parts, flat, stage, bias, last)
@@ -550,7 +631,7 @@
         att_ref[rows, :] = join_heads(mixed, heads32).astype(BF16)
         return carry
 
-    lax.fori_loop(0, WIN, attend, 0)
+    lax.fori_loop(0, WIN, attend, 0, unroll=True)
 
     for c in in_copies[1]:
         c.wait_recv()
@@ -582,7 +663,7 @@
         datt_ref[rows, :] = mm_nt(dbb, w_proj[...]).astype(BF16)
         return gain_sum + jnp.sum(d_normed * unit, axis=0, keepdims=True)
 
-    gain_sum2 = lax.fori_loop(0, 2, feed, jnp.zeros((1, C), F32))
+    gain_sum2 = lax.fori_loop(0, 2, feed, jnp.zeros((1, C), F32), unroll=True)
 
     early_pack[1152:EARLY, 128:256] = jnp.zeros((EARLY - 1152, 128), F32)
     early_pack[1344:EARLY, 0:128] = jnp.zeros((EARLY - 1344, 128), F32)
@@ -598,6 +679,7 @@
     )
     out_copies = send_out(0)
 
+    early.to_lon()
     d_bias[...] = jnp.zeros_like(d_bias)
 
     def attend_back(w, carry):
@@ -618,63 +700,78 @@
         dk_ref[rows, :] = (mm_tn(d_score_b, stacked) * scale).astype(BF16)
         return carry
 
-    lax.fori_loop(0, WIN // 2, attend_back, 0)
-    early.to_lon()
-    lax.fori_loop(WIN // 2, WIN, attend_back, 0)
+    lax.fori_loop(0, WIN, attend_back, 0, unroll=2)
+    pieces = EARLY // net.n_lon // 16
+    early.to_owner(pieces)
 
     d_normed = None
-    late_pack[:, 128:256] = jnp.zeros((LATE, 128), F32)
-    late_pack[576:LATE, 0:128] = jnp.zeros((LATE - 576, 128), F32)
+    late_pack[432:LATE, :] = jnp.zeros((LATE - 432, 256), F32)
     for i, ref in enumerate((dq_ref, dk_ref, dv_ref)):
-        late_pack[i * C : (i + 1) * C, 0:C] = mm_tn(n1_ref[...], ref[...])
+        grad = mm_tn(n1_ref[...], ref[...])
+        late_pack[i * TOK : (i + 1) * TOK, 0:C] = grad[0:TOK, :]
+        for j in range(3):
+            rows = slice(i * TOK + j * 48, i * TOK + (j + 1) * 48)
+            late_pack[rows, C:256] = grad[TOK:C, j * 64 : (j + 1) * 64]
         term = mm_nt(ref[...], w_qkv[:, i * C : (i + 1) * C])
         d_normed = term if d_normed is None else d_normed + term
     unit, inverse = norm(x_ref[...])
-    late_pack[576:577, 0:C] = jnp.sum(d_normed * unit, axis=0, keepdims=True)
+    late_pack[432:433, 0:C] = jnp.sum(d_normed * unit, axis=0, keepdims=True)
     out_ref[...] = dbranch_ref[...] + norm_grad(d_normed, gain1, unit, inverse)
     reduce_table(d_bias, here["spread"], parts, flat, table)
     late.to_pair()
-    early.to_lat()
+    early.from_owner(pieces)
     late.to_lon()
     scatter_all(
         out_ref, here["place_out"], here["pick_out"], own_out.at[1], full.at[1], edges_back.at[1]
     )
     out_copies += send_out(1)
-    early.spread_lon()
+    early.after_owner(pieces)
     late.to_lat()
-    late.spread_lon()
+    late.from_lat()
     early.spread_pair()
     late.spread_pair()
     early.close()
     late.close()
+    early.close_owner(pieces)
     for c in out_copies:
         c.wait_recv()
     for c in net.started:
         c.wait_send()
 
 
-def finish_kernel(
-    n_k,
-    early,
-    late,
-    own_out,
-    below_out,
-    edge_out,
-    place_end,
-    edge_end,
-    block_out,
-    grad_fields,
-    g_gain_one,
-    g_w_qkv,
-    g_table,
-    g_w_proj,
-    g_gain_two,
-    g_w_in,
-    g_w_out,
-    early_rows,
-    late_rows,
-):
+def finish_kernel(n_k, *refs):
+    hbm, outs, here = refs[0:7], refs[7:16], refs[16:23]
+    early_rows, late_rows = refs[23:25]
+    results = refs[25:34]
+    load_sem, store_sem = refs[34:36]
+    loads = [pltpu.make_async_copy(hbm[i], here[i], load_sem.at[i]) for i in range(7)]
+    for c in loads:
+        c.start()
+    early, late, own_out, below_out, edge_out, place_end, edge_end = here
+    block_out, grad_fields, g_gain_one, g_w_qkv, g_table, g_w_proj, g_gain_two, _, _ = results
+    out_w_in, out_w_out = outs[7], outs[8]
+    stores = []
+
+    def store(source, target):
+        c = pltpu.make_async_copy(source, target, store_sem.at[len(stores)])
+        c.start()
+        stores.append(c)
+
     n_lon = 2 * n_k
+    chunk = EARLY // n_lon
+    loads[0].wait()
+    for part in range(n_lon):
+        early_rows[part * chunk : (part + 1) * chunk, :] = early[part % 2, part // 2].astype(F32)
+    for i in range(3):
+        cols = slice(i * 256, (i + 1) * 256)
+        store(early_rows.at[i * C : (i + 1) * C, :], out_w_out.at[:, cols])
+        store(early_rows.at[576 + i * C : 576 + (i + 1) * C, :], out_w_in.at[:, cols])
+    g_w_proj[...] = early_rows[1152 : 1152 + C, 0:C]
+    store(g_w_proj, outs[5])
+    g_gain_two[...] = early_rows[1344:1345, 0:C]
+    store(g_gain_two, outs[6])
+    for c in loads[2:]:
+        c.wait()
     place = place_end[...].astype(BF16)
     for i, ref in enumerate((block_out, grad_fields)):
         for lev in range(4):
@@ -685,27 +782,30 @@
             rows = mm(place, jnp.concatenate(parts, axis=0).astype(BF16))
             rows = rows + mm(edge_end[lev].astype(BF16), edge_out[i])
             ref[(lev + 1) % 4] = rows.reshape(6, 24, C).astype(BF16)
-    for source, target, size in ((early, early_rows, EARLY), (late, late_rows, LATE)):
-        chunk = size // n_lon
-        for part in range(n_lon):
-            target[part * chunk : (part + 1) * chunk, :] = source[
-                part % 2, part // 2, 0:chunk, :
-            ].astype(F32)
+        store(ref, outs[i])
+    loads[1].wait()
+    rest, chunk = TABLE // n_lon, LATE // n_lon
+    for part in range(n_lon):
+        late_rows[part * chunk : (part + 1) * chunk, :] = late[
+            part % 2, part // 2, 0:chunk, :
+        ].astype(F32)
     for i in range(3):
-        cols = slice(i * 256, (i + 1) * 256)
-        g_w_out[:, cols] = early_rows[i * C : (i + 1) * C, :]
-        g_w_in[:, cols] = early_rows[576 + i * C : 576 + (i + 1) * C, :]
-        g_w_qkv[:, i * C : (i + 1) * C] = late_rows[i * C : (i + 1) * C, 0:C]
-    g_w_proj[...] = early_rows[1152 : 1152 + C, 0:C]
-    g_gain_two[...] = early_rows[1344:1345, 0:C]
-    g_gain_one[...] = late_rows[576:577, 0:C]
-    rest, chunk = TABLE // n_lon, LATE // n_lon
+        g_w_qkv[0:TOK, i * C : (i + 1) * C] = late_rows[i * TOK : (i + 1) * TOK, 0:C]
+        for j in range(3):
+            cols = slice(i * C + j * 64, i * C + (j + 1) * 64)
+            g_w_qkv[TOK:C, cols] = late_rows[i * TOK + j * 48 : i * TOK + (j + 1) * 48, C:256]
+    store(g_w_qkv, outs[3])
+    g_gain_one[...] = late_rows[432:433, 0:C]
+    store(g_gain_one, outs[2])
     for part in range(13):
         width = min(256, POS - part * 256)
         place, offset = divmod(part * 16, rest)
         value = late[place % 2, place // 2, chunk + offset : chunk + offset + 16, :].astype(F32)
         for h in range(HEADS):
             g_table[0, h, :, part * 256 : part * 256 + width] = value[2 * h : 2 * h + 2, 0:width]
+    store(g_table, outs[4])
+    for c in stores:
+        c.wait()
 
 
 def local(n_k, n_l, fields, cotangent, bias_table, gain_one, w_qkv, w_proj, gain_two, w_in, w_out):
@@ -745,6 +845,7 @@
             vmem((n_k - 1, chunk, 256), BF16),
             vmem((chunk, 256), F32),
             vmem((n_l, kept, 256), BF16),
+            vmem((n_l, 16, 256), BF16),
         ]
 
     slots = max(n_k, n_l)
@@ -793,39 +894,44 @@
             vmem((LATE, 256), F32),
             vmem((TABLE, 256), F32),
         ]
-        + buffers(early, early)
+        + buffers(early, 16)
         + buffers(both, late)
         + [
             dma((len(INPUTS),)),
             dma((2, 2, 3)),
             dma((2, 2, 3)),
-            dma((10, slots)),
-            dma((10, slots)),
+            dma((12, slots)),
+            dma((12, slots)),
         ],
         compiler_params=pltpu.CompilerParams(
             collective_id=0, has_side_effects=True, vmem_limit_bytes=60 * 1024 * 1024
         ),
         name="block",
     )(*inputs)
+    given = (*results, jnp.asarray(place_level_end()), jnp.asarray(place_edge_end()))
+    shapes = (
+        sds((4, 6, 24, C), BF16),
+        sds((4, 6, 24, C), BF16),
+        sds((1, C), F32),
+        sds((C, 3 * C), F32),
+        sds((1, HEADS, 2, POS), F32),
+        sds((C, C), F32),
+        sds((1, C), F32),
+        sds((C, FFH), F32),
+        sds((C, FFH), F32),
+    )
     outs = pl.pallas_call(
         functools.partial(finish_kernel, n_k),
-        out_shape=(
-            sds((4, 6, 24, C), BF16),
-            sds((4, 6, 24, C), BF16),
-            sds((1, C), F32),
-            sds((C, 3 * C), F32),
-            sds((1, HEADS, 2, POS), F32),
-            sds((C, C), F32),
-            sds((1, C), F32),
-            sds((C, FFH), F32),
-            sds((C, FFH), F32),
-        ),
-        in_specs=[whole] * 7,
-        out_specs=[whole] * 9,
-        scratch_shapes=[vmem((EARLY, 256), F32), vmem((LATE, 256), F32)],
+        out_shape=shapes,
+        in_specs=[apart] * 7,
+        out_specs=[apart] * 9,
+        scratch_shapes=[vmem(value.shape, value.dtype) for value in given]
+        + [vmem((EARLY, 256), F32), vmem((LATE, 256), F32)]
+        + [vmem(value.shape, value.dtype) for value in shapes]
+        + [dma((7,)), dma((13,))],
         compiler_params=pltpu.CompilerParams(vmem_limit_bytes=60 * 1024 * 1024),
         name="finish",
-    )(*results, jnp.asarray(place_level_end()), jnp.asarray(place_edge_end()))
+    )(*given)
     outs = list(outs)
     outs[2] = outs[2].reshape(C)
     outs[4] = outs[4].transpose(0, 2, 1, 3)

time: 70 us -> 68.1 us (0.973)
  Pallas kernels: 69.2 us -> 67.1 us
    pallas_call x1, Pallas kernels: 65.7 us -> 63.8 us  [local(): pl.pallas_call(functools.partial(block_kernel, n_k, n_l), out_shape=(sds(...]
where the time goes in v3:
time: 68.1 us; the launch traced here: 68 us
  Pallas kernels  67.1 us (99%)
  between operations  0.81 us (1%)
    pallas_call x1, Pallas kernels, local(): pl.pallas_call(functools.partial(block_kernel, n_k, n_l), out_shape=(sds(...  63.8 us
    pallas_call x1, Pallas kernels, local(): pl.pallas_call(functools.partial(finish_kernel, n_k), out_shape=shapes, i...  3.29 us

profile of v3, /device:TPU:1, one launch (start us, length us, event | category | flops | bytes accessed | tf_op | source)
XLA Modules:
  0.0 68.0 jit_solution(8128385222717138430)
XLA Ops:
  0.6 63.8 %block.1 = (bf16[2,8,96,256]{3,2,1,0:T(8,128)(2,1)}, bf16[2,8,48,256]{3,2,1,0:T(8,128)(2,1)}, bf16[2,4,3,24,192]{4,3,2,1,0:T(8,128)(2,1)}, bf16[2,4,3,24,192]{4,3,2,1,0:T(8,128)(2,1)}, bf16[2,160,192]{2,1,0:T(8,128)(2,1)}) custom-call(bf16[4,6,24,192]{3,2,1,0:T(8,128)(2,1)} %refs_0_.1, bf16[4,6,24,192]{3,2,1,0:T(8,128)(2,1)} %refs_1_.1, ...), custom_call_target="tpu_custom_call" | custom-call | tf_op jit(solution)/shard_map/block/pallas_call | solution.py:852
  64.5 3.3 %finish.1 = (bf16[4,6,24,192]{3,2,1,0:T(8,128)(2,1)}, bf16[4,6,24,192]{3,2,1,0:T(8,128)(2,1)}, f32[1,192]{1,0:T(1,128)}, f32[192,576]{1,0:T(8,128)}, f32[1,6,2,3...) custom-call(bf16[2,8,96,256]{3,2,1,0:T(8,128)(2,1)} %get-tuple-element.2, ...), custom_call_target="tpu_custom_call" | custom-call | tf_op jit(solution)/shard_map/finish/pallas_call | solution.py:923

commit v4 on v3

--- a/solution.py
+++ b/solution.py
@@ -17,7 +17,7 @@
 STACK = HEADS * TOK
 POS = 3312
 SEG = 138
-EARLY = 1536
+EARLY = 1280
 LATE = 512
 TABLE = 256
 EDGE = 80
@@ -276,6 +276,8 @@
     "spread",
     "masks",
     "heads",
+    "place_end",
+    "edge_end",
 )
 
 
@@ -524,9 +526,10 @@
         return out
 
     hbm = dict(zip(INPUTS, take(len(INPUTS)), strict=True))
-    early_out, late_out, own_out, below_out, edge_out = take(5)
+    early_out, late_out, block_out, grad_fields = take(4)
     here = dict(zip(INPUTS, take(len(INPUTS)), strict=True))
     below, edges, edges_send, full, edges_back = take(5)
+    own_out, below_out, edge_out = take(3)
     x_ref, cot_ref, n1_ref, q_ref, k_ref, v_ref, bias, probs, att_ref = take(9)
     act_ref, dpre_ref, n2_ref, dbb_ref, dbranch_ref, datt_ref, out_ref = take(7)
     dq_ref, dk_ref, dv_ref, d_bias, parts, stage, flat = take(7)
@@ -665,14 +668,19 @@
 
     gain_sum2 = lax.fori_loop(0, 2, feed, jnp.zeros((1, C), F32), unroll=True)
 
-    early_pack[1152:EARLY, 128:256] = jnp.zeros((EARLY - 1152, 128), F32)
-    early_pack[1344:EARLY, 0:128] = jnp.zeros((EARLY - 1344, 128), F32)
-    early_pack[1344:1345, 0:C] = gain_sum2
+    late_pack[448:LATE, :] = jnp.zeros((LATE - 448, 256), F32)
+    late_pack[456:457, 0:C] = gain_sum2
     for i in range(3):
         cols = slice(i * 256, (i + 1) * 256)
         early_pack[i * C : (i + 1) * C, :] = mm_tn(cot_ref[...], act_ref[:, cols])
         early_pack[576 + i * C : 576 + (i + 1) * C, :] = mm_tn(n2_ref[...], dpre_ref[:, cols])
-    early_pack[1152 : 1152 + C, 0:C] = mm_tn(att_ref[...], dbb_ref[...])
+    grad = mm_tn(att_ref[...], dbb_ref[...])
+    early_pack[1152:EARLY, 0:C] = grad[0:128, :]
+    late_pack[432:448, 0:C] = grad[128:TOK, :]
+    early_pack[1152:1200, C:256] = grad[TOK:C, 0:64]
+    early_pack[1200:1248, C:256] = grad[TOK:C, 64:128]
+    early_pack[1248:EARLY, C:256] = grad[TOK:176, 128:C]
+    late_pack[432:448, C:256] = grad[176:C, 128:C]
     early.to_pair()
     scatter_all(
         out_ref, here["place_out"], here["pick_out"], own_out.at[0], full.at[0], edges_back.at[0]
@@ -702,10 +710,8 @@
 
     lax.fori_loop(0, WIN, attend_back, 0, unroll=2)
     pieces = EARLY // net.n_lon // 16
-    early.to_owner(pieces)
 
     d_normed = None
-    late_pack[432:LATE, :] = jnp.zeros((LATE - 432, 256), F32)
     for i, ref in enumerate((dq_ref, dk_ref, dv_ref)):
         grad = mm_tn(n1_ref[...], ref[...])
         late_pack[i * TOK : (i + 1) * TOK, 0:C] = grad[0:TOK, :]
@@ -715,40 +721,54 @@
         term = mm_nt(ref[...], w_qkv[:, i * C : (i + 1) * C])
         d_normed = term if d_normed is None else d_normed + term
     unit, inverse = norm(x_ref[...])
-    late_pack[432:433, 0:C] = jnp.sum(d_normed * unit, axis=0, keepdims=True)
+    late_pack[448:449, 0:C] = jnp.sum(d_normed * unit, axis=0, keepdims=True)
     out_ref[...] = dbranch_ref[...] + norm_grad(d_normed, gain1, unit, inverse)
     reduce_table(d_bias, here["spread"], parts, flat, table)
     late.to_pair()
-    early.from_owner(pieces)
-    late.to_lon()
     scatter_all(
         out_ref, here["place_out"], here["pick_out"], own_out.at[1], full.at[1], edges_back.at[1]
     )
+    late.to_lon()
+    early.to_owner(pieces)
+
+    def merge(i, target):
+        for c in out_copies[3 * i : 3 * i + 3]:
+            c.wait_recv()
+        place = here["place_end"][...].astype(BF16)
+        for lev in range(4):
+            rows = [
+                below_out[i, lev].astype(F32).reshape(72, C),
+                own_out[i, lev].astype(F32).reshape(72, C),
+            ]
+            value = mm(place, jnp.concatenate(rows, axis=0).astype(BF16))
+            value = value + mm(here["edge_end"][lev].astype(BF16), edge_out[i])
+            target[(lev + 1) % 4] = value.reshape(6, 24, C).astype(BF16)
+
+    merge(0, block_out)
+    early.from_owner(pieces)
+    late.to_lat()
+    early.after_owner(pieces)
     out_copies += send_out(1)
-    early.after_owner(pieces)
-    late.to_lat()
     late.from_lat()
     early.spread_pair()
     late.spread_pair()
+    merge(1, grad_fields)
     early.close()
     late.close()
     early.close_owner(pieces)
-    for c in out_copies:
-        c.wait_recv()
     for c in net.started:
         c.wait_send()
 
 
 def finish_kernel(n_k, *refs):
-    hbm, outs, here = refs[0:7], refs[7:16], refs[16:23]
-    early_rows, late_rows = refs[23:25]
-    results = refs[25:34]
-    load_sem, store_sem = refs[34:36]
-    loads = [pltpu.make_async_copy(hbm[i], here[i], load_sem.at[i]) for i in range(7)]
+    hbm, outs, here = refs[0:4], refs[4:13], refs[13:17]
+    early_rows, late_rows = refs[17:19]
+    g_gain_one, g_w_qkv, g_table, g_w_proj, g_gain_two = refs[19:24]
+    load_sem, store_sem = refs[24:26]
+    loads = [pltpu.make_async_copy(hbm[i], here[i], load_sem.at[i]) for i in range(4)]
     for c in loads:
         c.start()
-    early, late, own_out, below_out, edge_out, place_end, edge_end = here
-    block_out, grad_fields, g_gain_one, g_w_qkv, g_table, g_w_proj, g_gain_two, _, _ = results
+    early, late = here[0:2]
     out_w_in, out_w_out = outs[7], outs[8]
     stores = []
 
@@ -766,23 +786,9 @@
         cols = slice(i * 256, (i + 1) * 256)
         store(early_rows.at[i * C : (i + 1) * C, :], out_w_out.at[:, cols])
         store(early_rows.at[576 + i * C : 576 + (i + 1) * C, :], out_w_in.at[:, cols])
-    g_w_proj[...] = early_rows[1152 : 1152 + C, 0:C]
-    store(g_w_proj, outs[5])
-    g_gain_two[...] = early_rows[1344:1345, 0:C]
-    store(g_gain_two, outs[6])
-    for c in loads[2:]:
-        c.wait()
-    place = place_end[...].astype(BF16)
-    for i, ref in enumerate((block_out, grad_fields)):
-        for lev in range(4):
-            parts = [
-                below_out[i, lev].astype(F32).reshape(72, C),
-                own_out[i, lev].astype(F32).reshape(72, C),
-            ]
-            rows = mm(place, jnp.concatenate(parts, axis=0).astype(BF16))
-            rows = rows + mm(edge_end[lev].astype(BF16), edge_out[i])
-            ref[(lev + 1) % 4] = rows.reshape(6, 24, C).astype(BF16)
-        store(ref, outs[i])
+    for i in range(2):
+        loads[2 + i].wait()
+        store(here[2 + i], outs[i])
     loads[1].wait()
     rest, chunk = TABLE // n_lon, LATE // n_lon
     for part in range(n_lon):
@@ -795,8 +801,17 @@
             cols = slice(i * C + j * 64, i * C + (j + 1) * 64)
             g_w_qkv[TOK:C, cols] = late_rows[i * TOK + j * 48 : i * TOK + (j + 1) * 48, C:256]
     store(g_w_qkv, outs[3])
-    g_gain_one[...] = late_rows[432:433, 0:C]
+    g_w_proj[0:128, :] = early_rows[1152:EARLY, 0:C]
+    g_w_proj[128:TOK, :] = late_rows[432:448, 0:C]
+    g_w_proj[TOK:C, 0:64] = early_rows[1152:1200, C:256]
+    g_w_proj[TOK:C, 64:128] = early_rows[1200:1248, C:256]
+    g_w_proj[TOK:176, 128:C] = early_rows[1248:EARLY, C:256]
+    g_w_proj[176:C, 128:C] = late_rows[432:448, C:256]
+    store(g_w_proj, outs[5])
+    g_gain_one[...] = late_rows[448:449, 0:C]
     store(g_gain_one, outs[2])
+    g_gain_two[...] = late_rows[456:457, 0:C]
+    store(g_gain_two, outs[6])
     for part in range(13):
         width = min(256, POS - part * 256)
         place, offset = divmod(part * 16, rest)
@@ -835,6 +850,8 @@
         jnp.asarray(spread_matrix()),
         jnp.asarray(region_masks()),
         jnp.asarray(head_masks()),
+        jnp.asarray(place_level_end()),
+        jnp.asarray(place_edge_end()),
     )
 
     def buffers(chunk, kept):
@@ -854,17 +871,19 @@
         out_shape=(
             sds((2, n_k, early, 256), BF16),
             sds((2, n_k, both, 256), BF16),
-            sds((2, 4, 3, 24, C), BF16),
-            sds((2, 4, 3, 24, C), BF16),
-            sds((2, 2 * EDGE, C), BF16),
+            sds((4, 6, 24, C), BF16),
+            sds((4, 6, 24, C), BF16),
         ),
         in_specs=[apart] * len(INPUTS),
-        out_specs=[whole] * 5,
+        out_specs=[whole] * 4,
         scratch_shapes=[vmem(value.shape, value.dtype) for value in inputs]
         + [
             vmem((2, 4, 3, 24, C), BF16),
             vmem((2, 2 * EDGE, C), BF16),
             vmem((2, 2 * EDGE, C), BF16),
+            vmem((2, 4, 3, 24, C), BF16),
+            vmem((2, 2 * EDGE, C), BF16),
+            vmem((2, 4, 3, 24, C), BF16),
             vmem((2, 4, 3, 24, C), BF16),
             vmem((2, 2 * EDGE, C), BF16),
             vmem((ROWS, C), F32),
@@ -908,7 +927,6 @@
         ),
         name="block",
     )(*inputs)
-    given = (*results, jnp.asarray(place_level_end()), jnp.asarray(place_edge_end()))
     shapes = (
         sds((4, 6, 24, C), BF16),
         sds((4, 6, 24, C), BF16),
@@ -923,15 +941,15 @@
     outs = pl.pallas_call(
         functools.partial(finish_kernel, n_k),
         out_shape=shapes,
-        in_specs=[apart] * 7,
+        in_specs=[apart] * 4,
         out_specs=[apart] * 9,
-        scratch_shapes=[vmem(value.shape, value.dtype) for value in given]
+        scratch_shapes=[vmem(value.shape, value.dtype) for value in results]
         + [vmem((EARLY, 256), F32), vmem((LATE, 256), F32)]
-        + [vmem(value.shape, value.dtype) for value in shapes]
-        + [dma((7,)), dma((13,))],
+        + [vmem(value.shape, value.dtype) for value in shapes[2:7]]
+        + [dma((4,)), dma((13,))],
         compiler_params=pltpu.CompilerParams(vmem_limit_bytes=60 * 1024 * 1024),
         name="finish",
-    )(*given)
+    )(*results)
     outs = list(outs)
     outs[2] = outs[2].reshape(C)
     outs[4] = outs[4].transpose(0, 2, 1, 3)

time: 68.1 us -> 64.1 us (0.941)
  Pallas kernels: 67.1 us -> 63.1 us
    pallas_call x1, Pallas kernels: 63.8 us -> 60.3 us  [local(): pl.pallas_call(functools.partial(block_kernel, n_k, n_l), out_shape=(sds(...]
where the time goes in v4:
time: 64.1 us; the launch traced here: 63.9 us
  Pallas kernels  63.1 us (98%)
  between operations  0.81 us (1%)
    pallas_call x1, Pallas kernels, local(): pl.pallas_call(functools.partial(block_kernel, n_k, n_l), out_shape=(sds(...  60.3 us
    pallas_call x1, Pallas kernels, local(): pl.pallas_call(functools.partial(finish_kernel, n_k), out_shape=shapes, i...  2.8 us

profile of v4, /device:TPU:1, one launch (start us, length us, event | category | flops | bytes accessed | tf_op | source)
XLA Modules:
  0.0 63.9 jit_solution(3703539431441135639)
XLA Ops:
  0.6 60.3 %block.1 = (bf16[2,8,80,256]{3,2,1,0:T(8,128)(2,1)}, bf16[2,8,48,256]{3,2,1,0:T(8,128)(2,1)}, bf16[4,6,24,192]{3,2,1,0:T(8,128)(2,1)}, bf16[4,6,24,192]{3,2,1,0:T(8,128)(2,1)}) custom-call(bf16[4,6,24,192]{3,2,1,0:T(8,128)(2,1)} %refs_0_.1, bf16[4,6,24,192]{3,2,1,0:T(8,128)(2,1)} %refs_1_.1, f32[1,6,2,3312]{3,2,1,0:T(2,128)} %bitcast.9, f32[1,192]{1,0:T(1,128)} %bitcast.10, ...), custom_call_target="tpu_custom_call" | custom-call | tf_op jit(solution)/shard_map/block/pallas_call | solution.py:869
  61.0 2.8 %finish.1 = (bf16[4,6,24,192]{3,2,1,0:T(8,128)(2,1)}, bf16[4,6,24,192]{3,2,1,0:T(8,128)(2,1)}, f32[1,192]{1,0:T(1,128)}, f32[192,576]{1,0:T(8,128)}, f32[1,6,2,3...) custom-call(bf16[2,8,80,256]{3,2,1,0:T(8,128)(2,1)} %get-tuple-element.2, ...), custom_call_target="tpu_custom_call" | custom-call | tf_op jit(solution)/shard_map/finish/pallas_call | solution.py:941

commit v5 on v4

--- a/solution.py
+++ b/solution.py
@@ -730,6 +730,7 @@
     )
     late.to_lon()
     early.to_owner(pieces)
+    out_copies += send_out(1)
 
     def merge(i, target):
         for c in out_copies[3 * i : 3 * i + 3]:
@@ -748,7 +749,6 @@
     early.from_owner(pieces)
     late.to_lat()
     early.after_owner(pieces)
-    out_copies += send_out(1)
     late.from_lat()
     early.spread_pair()
     late.spread_pair()

time: 64.1 us -> 61.9 us (0.966)
  Pallas kernels: 63.1 us -> 61 us
    pallas_call x1, Pallas kernels: 60.3 us -> 58.2 us  [local(): pl.pallas_call(functools.partial(block_kernel, n_k, n_l), out_shape=(sds(...]
where the time goes in v5:
time: 61.9 us; the launch traced here: 61.8 us
  Pallas kernels  61 us (99%)
  between operations  0.81 us (1%)
    pallas_call x1, Pallas kernels, local(): pl.pallas_call(functools.partial(block_kernel, n_k, n_l), out_shape=(sds(...  58.2 us
    pallas_call x1, Pallas kernels, local(): pl.pallas_call(functools.partial(finish_kernel, n_k), out_shape=shapes, i...  2.8 us

profile of v5, /device:TPU:1, one launch (start us, length us, event | category | flops | bytes accessed | tf_op | source)
XLA Modules:
  0.0 61.8 jit_solution(6905283574084791714)
XLA Ops:
  0.6 58.2 %block.1 = (bf16[2,8,80,256]{3,2,1,0:T(8,128)(2,1)}, bf16[2,8,48,256]{3,2,1,0:T(8,128)(2,1)}, bf16[4,6,24,192]{3,2,1,0:T(8,128)(2,1)}, bf16[4,6,24,192]{3,2,1,0:T(8,128)(2,1)}) custom-call(bf16[4,6,24,192]{3,2,1,0:T(8,128)(2,1)} %refs_0_.1, bf16[4,6,24,192]{3,2,1,0:T(8,128)(2,1)} %refs_1_.1, f32[1,6,2,3312]{3,2,1,0:T(2,128)} %bitcast.9, f32[1,192]{1,0:T(1,128)} %bitcast.10, ...), custom_call_target="tpu_custom_call" | custom-call | tf_op jit(solution)/shard_map/block/pallas_call | solution.py:869
  58.8 2.8 %finish.1 = (bf16[4,6,24,192]{3,2,1,0:T(8,128)(2,1)}, bf16[4,6,24,192]{3,2,1,0:T(8,128)(2,1)}, f32[1,192]{1,0:T(1,128)}, f32[192,576]{1,0:T(8,128)}, f32[1,6,2,3...) custom-call(bf16[2,8,80,256]{3,2,1,0:T(8,128)(2,1)} %get-tuple-element.2, ...), custom_call_target="tpu_custom_call" | custom-call | tf_op jit(solution)/shard_map/finish/pallas_call | solution.py:941

commit v6 on v5

--- a/solution.py
+++ b/solution.py
@@ -554,48 +554,49 @@
         [late_pack, table, *late_bufs, late_out, late_sem],
     )
 
+    def pick_in(i, name):
+        flat_rows = here[name][...].astype(F32).reshape(ROWS, C).astype(BF16)
+        edges_send[i] = mm(here["pick_in"][...].astype(BF16), flat_rows).astype(BF16)
+
     def send_in(i, name):
+        corner = net.start(
+            edges_send.at[i, EDGE : 2 * EDGE],
+            edges.at[i, EDGE : 2 * EDGE],
+            (in_sem.at[0, i, 2], in_sem.at[1, i, 2]),
+            net.at(-1, -1),
+        )
         south = net.start(
             hbm[name].at[:, 0:3], below.at[i], (in_sem.at[0, i, 0], in_sem.at[1, i, 0]), net.at(0, -1)
         )
-        if i == 0:
-            loads["fields"].wait()
-            loads["pick_in"].wait()
-        flat_rows = here[name][...].astype(F32).reshape(ROWS, C).astype(BF16)
-        edges_send[i] = mm(here["pick_in"][...].astype(BF16), flat_rows).astype(BF16)
         east = net.start(
             edges_send.at[i, 0:EDGE],
             edges.at[i, 0:EDGE],
             (in_sem.at[0, i, 1], in_sem.at[1, i, 1]),
             net.at(-1, 0),
         )
+        return [south, east, corner]
+
+    def send_out(i):
         corner = net.start(
-            edges_send.at[i, EDGE : 2 * EDGE],
-            edges.at[i, EDGE : 2 * EDGE],
-            (in_sem.at[0, i, 2], in_sem.at[1, i, 2]),
-            net.at(-1, -1),
+            edges_back.at[i, EDGE : 2 * EDGE],
+            edge_out.at[i, EDGE : 2 * EDGE],
+            (out_sem.at[0, i, 2], out_sem.at[1, i, 2]),
+            net.at(1, 1),
         )
-        return [south, east, corner]
-
-    def send_out(i):
-        return [
-            net.start(
-                full.at[i], below_out.at[i], (out_sem.at[0, i, 0], out_sem.at[1, i, 0]), net.at(0, 1)
-            ),
-            net.start(
-                edges_back.at[i, 0:EDGE],
-                edge_out.at[i, 0:EDGE],
-                (out_sem.at[0, i, 1], out_sem.at[1, i, 1]),
-                net.at(1, 0),
-            ),
-            net.start(
-                edges_back.at[i, EDGE : 2 * EDGE],
-                edge_out.at[i, EDGE : 2 * EDGE],
-                (out_sem.at[0, i, 2], out_sem.at[1, i, 2]),
-                net.at(1, 1),
-            ),
-        ]
-
+        north = net.start(
+            full.at[i], below_out.at[i], (out_sem.at[0, i, 0], out_sem.at[1, i, 0]), net.at(0, 1)
+        )
+        west = net.start(
+            edges_back.at[i, 0:EDGE],
+            edge_out.at[i, 0:EDGE],
+            (out_sem.at[0, i, 1], out_sem.at[1, i, 1]),
+            net.at(1, 0),
+        )
+        return [north, west, corner]
+
+    loads["fields"].wait()
+    loads["pick_in"].wait()
+    pick_in(0, "fields")
     pl.semaphore_wait(barrier, count)
     in_copies = [send_in(0, "fields")]
     for name in INPUTS:
@@ -605,6 +606,7 @@
     last = (net.lat == n_l - 1).astype(F32)
     expand_bias(here["bias_table"], here["spread"], here["masks"], parts, flat, stage, bias, last)
 
+    pick_in(1, "cotangent")
     heads32 = here["heads"][...]
     heads = heads32.astype(BF16)
     scale = 32**-0.5

time: 61.9 us -> 60 us (0.969)
  Pallas kernels: 61 us -> 59 us
    pallas_call x1, Pallas kernels: 58.2 us -> 56.2 us  [local(): pl.pallas_call(functools.partial(block_kernel, n_k, n_l), out_shape=(sds(...]
where the time goes in v6:
time: 60 us; the launch traced here: 59.9 us
  Pallas kernels  59 us (98%)
  between operations  0.81 us (1%)
    pallas_call x1, Pallas kernels, local(): pl.pallas_call(functools.partial(block_kernel, n_k, n_l), out_shape=(sds(...  56.2 us
    pallas_call x1, Pallas kernels, local(): pl.pallas_call(functools.partial(finish_kernel, n_k), out_shape=shapes, i...  2.8 us

profile of v6, /device:TPU:1, one launch (start us, length us, event | category | flops | bytes accessed | tf_op | source)
XLA Modules:
  0.0 59.9 jit_solution(8040016059357540637)
XLA Ops:
  0.6 56.2 %block.1 = (bf16[2,8,80,256]{3,2,1,0:T(8,128)(2,1)}, bf16[2,8,48,256]{3,2,1,0:T(8,128)(2,1)}, bf16[4,6,24,192]{3,2,1,0:T(8,128)(2,1)}, bf16[4,6,24,192]{3,2,1,0:T(8,128)(2,1)}) custom-call(bf16[4,6,24,192]{3,2,1,0:T(8,128)(2,1)} %refs_0_.1, bf16[4,6,24,192]{3,2,1,0:T(8,128)(2,1)} %refs_1_.1, f32[1,6,2,3312]{3,2,1,0:T(2,128)} %bitcast.9, f32[1,192]{1,0:T(1,128)} %bitcast.10, ...), custom_call_target="tpu_custom_call" | custom-call | tf_op jit(solution)/shard_map/block/pallas_call | solution.py:871
  56.9 2.8 %finish.1 = (bf16[4,6,24,192]{3,2,1,0:T(8,128)(2,1)}, bf16[4,6,24,192]{3,2,1,0:T(8,128)(2,1)}, f32[1,192]{1,0:T(1,128)}, f32[192,576]{1,0:T(8,128)}, f32[1,6,2,3...) custom-call(bf16[2,8,80,256]{3,2,1,0:T(8,128)(2,1)} %get-tuple-element.2, ...), custom_call_target="tpu_custom_call" | custom-call | tf_op jit(solution)/shard_map/finish/pallas_call | solution.py:943

commit v7 on v6

--- a/solution.py
+++ b/solution.py
@@ -599,14 +599,16 @@
     pick_in(0, "fields")
     pl.semaphore_wait(barrier, count)
     in_copies = [send_in(0, "fields")]
+    loads["cotangent"].wait()
+    pick_in(1, "cotangent")
+    in_copies.append(send_in(1, "cotangent"))
     for name in INPUTS:
-        if name not in ("fields", "pick_in"):
+        if name not in ("fields", "cotangent", "pick_in"):
             loads[name].wait()
 
     last = (net.lat == n_l - 1).astype(F32)
     expand_bias(here["bias_table"], here["spread"], here["masks"], parts, flat, stage, bias, last)
 
-    pick_in(1, "cotangent")
     heads32 = here["heads"][...]
     heads = heads32.astype(BF16)
     scale = 32**-0.5
@@ -616,7 +618,6 @@
 
     for c in in_copies[0]:
         c.wait_recv()
-    in_copies.append(send_in(1, "cotangent"))
     gather_all(here["fields"], below.at[0], edges.at[0], here["place_in"], here["edge_in"], x_ref)
     unit, _ = norm(x_ref[...])
     n1 = (unit * gain1).astype(BF16)

time: 60 us -> 58.4 us (0.973)
  Pallas kernels: 59 us -> 57.5 us
    pallas_call x1, Pallas kernels: 56.2 us -> 54.7 us  [local(): pl.pallas_call(functools.partial(block_kernel, n_k, n_l), out_shape=(sds(...]
where the time goes in v7:
time: 58.4 us; the launch traced here: 58.3 us
  Pallas kernels  57.5 us (98%)
  between operations  0.81 us (1%)
    pallas_call x1, Pallas kernels, local(): pl.pallas_call(functools.partial(block_kernel, n_k, n_l), out_shape=(sds(...  54.7 us
    pallas_call x1, Pallas kernels, local(): pl.pallas_call(functools.partial(finish_kernel, n_k), out_shape=shapes, i...  2.8 us

profile of v7, /device:TPU:1, one launch (start us, length us, event | category | flops | bytes accessed | tf_op | source)
XLA Modules:
  0.0 58.3 jit_solution(13856131314696361729)
XLA Ops:
  0.6 54.7 %block.1 = (bf16[2,8,80,256]{3,2,1,0:T(8,128)(2,1)}, bf16[2,8,48,256]{3,2,1,0:T(8,128)(2,1)}, bf16[4,6,24,192]{3,2,1,0:T(8,128)(2,1)}, bf16[4,6,24,192]{3,2,1,0:T(8,128)(2,1)}) custom-call(bf16[4,6,24,192]{3,2,1,0:T(8,128)(2,1)} %refs_0_.1, bf16[4,6,24,192]{3,2,1,0:T(8,128)(2,1)} %refs_1_.1, f32[1,6,2,3312]{3,2,1,0:T(2,128)} %bitcast.9, f32[1,192]{1,0:T(1,128)} %bitcast.10, ...), custom_call_target="tpu_custom_call" | custom-call | tf_op jit(solution)/shard_map/block/pallas_call | solution.py:872
  55.3 2.8 %finish.1 = (bf16[4,6,24,192]{3,2,1,0:T(8,128)(2,1)}, bf16[4,6,24,192]{3,2,1,0:T(8,128)(2,1)}, f32[1,192]{1,0:T(1,128)}, f32[192,576]{1,0:T(8,128)}, f32[1,6,2,3...) custom-call(bf16[2,8,80,256]{3,2,1,0:T(8,128)(2,1)} %get-tuple-element.2, ...), custom_call_target="tpu_custom_call" | custom-call | tf_op jit(solution)/shard_map/finish/pallas_call | solution.py:944
